TPU v7x, 512 devices: a whole 4x8x8 slice. The times are simulated.
512 devices in a mesh: expert: 8 (over z_lo, core), dp: 64 (over x, y, z_hi).
Axes of the slice: x: 4, y: 8, z: 8 (z_hi: 2, z_lo: 4; z = z_hi * 4 + z_lo), core: 2. Of those that a mesh axis runs over, the one named last changes fastest.
Arguments:
- features: bfloat16 [65536, 512], P(('expert', 'dp')), may hold values from -31 to 31
- gradients: bfloat16 [65536, 512], P(('expert', 'dp')), may hold values from -31 to 31
- route_ids: int32 [65536, 2], P(('expert', 'dp')), may hold values from 0 to 7, all different within a row; in each aligned block of 128 rows (0 to 127, 128 to 255, ...) at most 64 rows name the same one
- gate_share: float32 [65536], P(('expert', 'dp')), may hold values from 0.5 to 0.95
- token_mask: int32 [65536], P(('expert', 'dp')), may hold values 0 or 1
- damping: float32 [8, 2, 1], P('expert'), may hold values from 0.5 to 2
Outputs:
- act_inverse: float32 [8, 1, 512, 512], P(None, None, 'dp')
- grad_inverse: float32 [8, 1, 512, 512], P(None, None, 'dp')
Inputs may be any that keep to these rules, and one draw needn't show every extreme that they name: `route_ids`: each token names two different experts. Among the 128 tokens of one device no expert is named by more than 64 tokens, a bound that some block reaches.
All inputs are finite; a program needn't handle non-finite values. Where the computation divides by a largest or mean magnitude, that divisor is 1e-20 or more. No bound on the sum of `token_mask` on one device may be relied on, other than what follows from the above.
Results may differ from a plain program's by a relative error of at most 0.0003.
Values may be sent and summed in bfloat16 or wider, within the bound.
A program may use at most 64 MiB of HBM per device.

v0:
```python
import jax
import jax.numpy as jnp
from jax import lax
from jax.sharding import PartitionSpec as P

EXPERTS = 8
TOP = 2
BLOCK = 512
NBLK = 1
CAP = 64
WIDTH = 512


def padded_to(lines, devices):
    spare = -len(lines) % devices
    return jnp.pad(lines, [(0, spare)] + [(0, 0)] * (lines.ndim - 1))


def in_order(parts, dim):
    parts = jnp.moveaxis(parts, 0, dim)
    dims = parts.shape
    return parts.reshape(*dims[:dim], dims[dim] * dims[dim + 1], *dims[dim + 2 :])


def sent_to_all(value, axis):
    copies = jnp.broadcast_to(value, (lax.axis_size(axis), *value.shape))
    return lax.all_to_all(copies, axis, split_axis=0, concat_axis=0, tiled=True)


def gathered_copies(value, axis, dim):
    return in_order(sent_to_all(value, axis), dim)


def in_blocks(value, dim, devices):
    dims = value.shape
    parts = value.reshape(*dims[:dim], devices, dims[dim] // devices, *dims[dim + 1 :])
    return jnp.moveaxis(parts, dim, 0)


def sent_and_summed(value, axis, dim):
    devices = lax.axis_size(axis)
    parts = lax.all_to_all(in_blocks(value, dim, devices), axis, 0, 0, tiled=True)
    return jnp.sum(parts, axis=0)


def total_of(value, axes):
    padded = padded_to(value, lax.axis_size(axes))
    whole = gathered_copies(sent_and_summed(padded, axes, 0), axes, 0)
    return lax.slice_in_dim(whole, 0, len(value)).reshape(value.shape)


def packed_total(arrays, axis):
    ravelled, at, finished = (jnp.concatenate([a.reshape(-1) for a in arrays]), 0, [])
    so_far = total_of(ravelled, axis)
    for a in arrays:
        finished.append(so_far[at : at + a.size].reshape(a.shape))
        at += a.size
    return tuple(finished)


def in_one_piece(arrays, axis, dim, along):
    both = jnp.concatenate(arrays, axis=along)
    whole, at, finished = (lax.all_gather(both, axis, axis=dim, tiled=True), 0, [])
    for a in arrays:
        finished.append(lax.slice_in_dim(whole, at, at + a.shape[along], axis=along))
        at += a.shape[along]
    return tuple(finished)


def slot_table(route_ids, capacity):
    pair_experts = route_ids.reshape(-1)
    onehot = (pair_experts[:, None] == jnp.arange(EXPERTS, dtype=jnp.int32)[None, :]).astype(
        jnp.int32
    )
    running = jnp.cumsum(onehot, axis=0)
    position = jnp.sum(onehot * running, axis=1) - 1
    target = pair_experts * capacity + position
    sources = jnp.arange(1, pair_experts.shape[0] + 1, dtype=jnp.int32)
    return jnp.zeros((EXPERTS * capacity,), jnp.int32).at[target].set(sources)


def newton_rows(rows_now, matrix, whole_now):
    left_product = jnp.einsum("eirk,eikc->eirc", rows_now, matrix, precision=lax.Precision.HIGHEST)
    return 2.0 * rows_now - jnp.einsum(
        "eirk,eikc->eirc", left_product, whole_now, precision=lax.Precision.HIGHEST
    )


def first_iterate(matrix, identity, inverse_bound):
    bound_scale = inverse_bound[:, :, None, None]
    return 2.0 * bound_scale * identity - bound_scale * bound_scale * matrix


def fold_pack(blocks_full, half):
    corner = blocks_full[:, :, :half, half:]
    upper_left = blocks_full[:, :, :half, :half]
    lower_right = jnp.swapaxes(blocks_full[:, :, half:, half:], 2, 3)
    zero_row = jnp.zeros(blocks_full.shape[:2] + (1, half), jnp.float32)
    top_part = jnp.concatenate([upper_left, zero_row], axis=2)
    low_part = jnp.concatenate([zero_row, lower_right], axis=2)
    row_ids = lax.broadcasted_iota(jnp.int32, (half + 1, half), 0)
    col_ids = lax.broadcasted_iota(jnp.int32, (half + 1, half), 1)
    folded = jnp.where(row_ids <= col_ids, top_part, low_part)
    return (corner, folded)


def fold_unpack(corner, folded, half):
    row_ids = lax.broadcasted_iota(jnp.int32, (half, half), 0)
    col_ids = lax.broadcasted_iota(jnp.int32, (half, half), 1)
    head = folded[:, :, :half, :]
    upper_left = jnp.where(row_ids <= col_ids, head, jnp.swapaxes(head, 2, 3))
    tail = folded[:, :, 1:, :]
    lower_right = jnp.where(row_ids >= col_ids, tail, jnp.swapaxes(tail, 2, 3))
    top_rows = jnp.concatenate([upper_left, corner], axis=3)
    low_rows = jnp.concatenate([jnp.swapaxes(corner, 2, 3), lower_right], axis=3)
    return jnp.concatenate([top_rows, low_rows], axis=2)


def on_device(features, gradients, route_ids, gate_share, token_mask, damping):
    tokens_here = features.shape[0]
    capacity = CAP
    blocks = 2 * NBLK
    kept_mask = token_mask.astype(jnp.float32)
    weight_pair = jnp.stack([gate_share, 1.0 - gate_share], axis=1) * kept_mask[:, None]
    kept_rows = features * token_mask.astype(jnp.bfloat16)[:, None]
    pair_grads = (gradients[:, None, :].astype(jnp.float32) * weight_pair[:, :, None]).astype(
        jnp.bfloat16
    )
    repeated = jnp.broadcast_to(kept_rows[:, None, :], pair_grads.shape)
    pair_rows = jnp.concatenate([repeated, pair_grads], axis=2).reshape(
        tokens_here * TOP, 2 * WIDTH
    )
    padded = jnp.concatenate([jnp.zeros((1, 2 * WIDTH), jnp.bfloat16), pair_rows], axis=0)
    buffer = jnp.take(padded, slot_table(route_ids, capacity), axis=0).reshape(
        EXPERTS, capacity, blocks, BLOCK
    )
    load_inverse = 1.0 / (
        tokens_here * lax.axis_size("expert") * lax.axis_size("dp") * TOP / EXPERTS
    )
    received = lax.all_to_all(buffer, "expert", split_axis=0, concat_axis=1, tiled=True)
    gram_blocks = (
        jnp.einsum("erib,eric->eibc", received, received, preferred_element_type=jnp.float32)
        * load_inverse
    )
    damping_flat = damping.reshape(damping.shape[0], blocks)[:, :, None, None]
    rows_share = BLOCK // lax.axis_size("dp")
    row_start = lax.axis_index("dp") * rows_share
    identity = jnp.eye(BLOCK, dtype=jnp.float32)
    half = BLOCK // 2
    corner, folded = fold_pack(gram_blocks, half)
    corner_sum, folded_sum = packed_total((corner, folded), "dp")
    summed = fold_unpack(corner_sum, folded_sum, half)
    matrix = summed + damping_flat * identity
    largest_sum = jnp.max(jnp.sum(jnp.abs(matrix), axis=3), axis=2)
    inverse_bound = 1.0 / largest_sum
    iterate_one = first_iterate(matrix, identity, inverse_bound)
    iterate_two = newton_rows(iterate_one, matrix, iterate_one)
    second_rows = lax.dynamic_slice_in_dim(iterate_two, row_start, rows_share, 2)
    third_rows = newton_rows(second_rows, matrix, iterate_two)
    act_rows = third_rows[:, :NBLK]
    grad_rows = third_rows[:, NBLK:]
    act_inverse, grad_inverse = in_one_piece((act_rows, grad_rows), "expert", 0, 1)
    return (act_inverse, grad_inverse)


def solution(mesh):
    placed = (
        P(("expert", "dp"), None),
        P(("expert", "dp"), None),
        P(("expert", "dp"), None),
        P(("expert", "dp")),
        P(("expert", "dp")),
        P("expert", None, None),
    )
    return jax.shard_map(
        on_device,
        mesh=mesh,
        in_specs=placed,
        out_specs=(P(None, None, "dp", None), P(None, None, "dp", None)),
        check_vma=False,
    )
```

profile of v0, /device:TPU:1, one launch (start us, length us, event | category | flops | bytes accessed | tf_op | source)
XLA Modules:
  0.0 180.9 jit_solution(5684483519095609114)
XLA Ops:
  3.6 1.4 scatter_custom_fusion
  7.6 1.0 mul.169
  9.7 2.1 %gather_fusion = bf16[512,1024]{1,0:T(8,128)(2,1)S(1)} fusion(bf16[257,1024]{1,0:T(8,128)(2,1)S(1)} %fusion.13, s32[1024]{0:T(1024)S(1)} %pad_clamp_fusion), kind=kCustom, calls=%fused_computation | custom fusion | bytes 2099200 | tf_op jit(solution)/shard_map/jit(_take)/gather | solution.py:134
  12.6 1.2 copy_select_fusion
  13.8 10.3 %all-to-all-start = ((bf16[8,64,2,512]{3,1,2,0:T(8,128)(2,1)}), bf16[8,64,2,512]{3,1,2,0:T(8,128)(2,1)S(1)}, u32[]{:S(2)}, u32[]{:S(2)}) async-start(bf16[8,64,2,512]{3,1,2,0:T(8,128)(2,1)} %copy_select_fusion), calls=%async_computation | async-start | bytes 2097152 | tf_op jit(solution)/shard_map/all_to_all | solution.py:140
  24.2 25.7 %all-to-all-done = bf16[8,64,2,512]{3,1,2,0:T(8,128)(2,1)S(1)} async-done(((bf16[8,64,2,512]{3,1,2,0:T(8,128)(2,1)}), bf16[8,64,2,512]{3,1,2,0:T(8,128)(2,1)S(1)}, u32[]{:S(2)}, u32[]{:S(2)}) %all-to-all-start) | async-done | bytes 1048608 | tf_op jit(solution)/shard_map/all_to_all | solution.py:140
  52.0 1.4 all_to_all.18
  53.4 45.6 %all_to_all.24 = f32[64,1,4104]{2,1,0:T(1,128)S(1)} all-to-all(f32[64,1,4104]{2,1,0:T(1,128)S(1)} %all_to_all.18), channel_id=1, replica_groups=mesh['expert'=8,'dp'=64] {'dp'}, dimensions={0} | all-to-all | bytes 2101248 | tf_op jit(solution)/shard_map/all_to_all | solution.py:42
  99.6 1.5 broadcast_in_dim.56
  101.2 8.0 %all-to-all-start.2 = ((f32[64,1,4104]{2,1,0:T(1,128)}), f32[64,1,4104]{2,1,0:T(1,128)S(1)}, u32[]{:S(2)}, u32[]{:S(2)}) async-start(f32[64,1,4104]{2,1,0:T(1,128)} %broadcast_in_dim.56), calls=%async_computation.2 | async-start | bytes 2162688 | tf_op jit(solution)/shard_map/all_to_all | solution.py:27
  109.3 31.0 %all-to-all-done.2 = f32[64,1,4104]{2,1,0:T(1,128)S(1)} async-done(((f32[64,1,4104]{2,1,0:T(1,128)}), f32[64,1,4104]{2,1,0:T(1,128)S(1)}, u32[]{:S(2)}, u32[]{:S(2)}) %all-to-all-start.2) | async-done | bytes 1050656 | tf_op jit(solution)/shard_map/all_to_all | solution.py:27
  140.4 2.6 %reduce.5 = f32[64,4104]{1,0:T(8,128)S(1)} reduce(f32[64,1,4104]{2,1,0:T(1,128)S(1)} %all-to-all-done.2, f32[]{:T(128)} %constant.67), dimensions={1}, to_apply=%all_to_all.20.reduce_sub_computation | reduce | bytes 2101252 | tf_op jit(solution)/shard_map/all_to_all | solution.py:27
  143.5 0.9 copy-done.3
  144.5 0.9 fusion.22
  145.4 1.2 copy.74
  146.7 1.0 copy.75
  147.9 1.0 copy.70
  148.9 1.2 bitcast_select_fusion.1
  150.1 1.3 maximum_bitcast_fusion
  152.1 4.1 %fusion.3 = f32[2,512,512]{2,1,0:T(8,128)S(1)} fusion(f32[2]{0:T(128)S(1)} %mul.187, f32[512,512]{1,0:T(8,128)S(1)} %fusion.12, f32[2]{0:T(128)S(1)} %get-tuple-element.2, f32[2,256,512]{2,1,0:T(8,128)S(1)} %get-tuple-element.16, f32[2,256,512]{2,1,0:T(8,128)S(1)} %get-tuple-element.15, f32[2]{0:T(128)S(1)} %bitcast.42), kind=kOutput, calls=%fused_computation.9 | convolution fusion | flops 3225944064 | bytes 5242904 | tf_op jit(solution)/shard_map/eirk,eikc->eirc/dot_general | solution.py:83
  156.2 4.5 %multiply_subtract_fusion = f32[2,512,512]{2,1,0:T(8,128)S(1)} fusion(f32[2,512,512]{2,1,0:T(8,128)S(1)} %fusion.3, f32[2]{0:T(128)S(1)} %mul.187, f32[512,512]{1,0:T(8,128)S(1)} %fusion.12, f32[2]{0:T(128)S(1)} %get-tuple-element.2, f32[2]{0:T(128)S(1)} %bitcast.43, f32[2,256,512]{2,1,0:T(8,128)S(1)} %get-tuple-element.16, ...), kind=kOutput, calls=%fused_computation.6 | convolution fusion | flops 3228565504 | bytes 7340056 | tf_op jit(solution)/shard_map/eirk,eikc->eirc/dot_general | solution.py:84
  160.7 1.3 fusion.14
  162.0 1.1 convolution_subtract_fusion
  163.1 17.1 %all-gather = f32[16,8,512]{2,1,0:T(8,128)S(1)} all-gather(f32[2,8,512]{2,1,0:T(8,128)S(1)} %convolution_subtract_fusion), channel_id=2, replica_groups=mesh['expert'=8,'dp'=64] {'expert'}, dimensions={0}, use_global_device_ids=true | all-gather | bytes 294912 | tf_op jit(solution)/shard_map/all_gather | solution.py:63
  (70 shorter events, 12.4 us)
Async XLA Ops:
  0.6 8.4 %copy-start.4 = (bf16[128,512]{1,0:T(8,128)(2,1)S(1)}, bf16[128,512]{1,0:T(8,128)(2,1)}, u32[]{:S(2)}) copy-start(bf16[128,512]{1,0:T(8,128)(2,1)} %param.6) | copy-start | bytes 393220
  13.8 36.1 %all-to-all-start = ((bf16[8,64,2,512]{3,1,2,0:T(8,128)(2,1)}), bf16[8,64,2,512]{3,1,2,0:T(8,128)(2,1)S(1)}, u32[]{:S(2)}, u32[]{:S(2)}) async-start(bf16[8,64,2,512]{3,1,2,0:T(8,128)(2,1)} %copy_select_fusion), calls=%async_computation | async-start | bytes 2097152 | tf_op jit(solution)/shard_map/all_to_all | solution.py:140
  101.2 39.2 %all-to-all-start.2 = ((f32[64,1,4104]{2,1,0:T(1,128)}), f32[64,1,4104]{2,1,0:T(1,128)S(1)}, u32[]{:S(2)}, u32[]{:S(2)}) async-start(f32[64,1,4104]{2,1,0:T(1,128)} %broadcast_in_dim.56), calls=%async_computation.2 | async-start | bytes 2162688 | tf_op jit(solution)/shard_map/all_to_all | solution.py:27
  143.4 1.0 copy-start.3
  144.5 3.2 %slice-start = ((f32[262656]{0:T(1024)}), f32[131072]{0:T(1024)S(1)}, s32[]{:S(2)}) async-start(f32[262656]{0:T(1024)} %copy-done.3), calls=%async_computation.3 | async-start | bytes 1048576 | tf_op jit(solution)/shard_map/slice | solution.py:56
  147.8 2.2 %copy-start = (f32[1,2,256,256]{3,2,1,0:T(8,128)}, f32[1,2,256,256]{3,2,1,0:T(8,128)S(1)}, u32[]{:S(2)}) copy-start(f32[1,2,256,256]{3,2,1,0:T(8,128)S(1)} %reshape.260) | copy-start | bytes 1572868
  148.9 1.2 copy-start.2
  150.1 1.4 copy-start.1
  150.1 1.4 copy-start.5
where the time goes:
time: 181 us
  blocking collectives  62.7 us (35%)
  waiting for transfers between devices  56.8 us (31%)
  local copies, waits for them, and re-layouts  18.5 us (10%)
  starting transfers between devices  18.3 us (10%)
  other arithmetic  11.9 us (7%)
  matrix products  11.7 us (6%)
    all_to_all x1, blocking collectives, sent_and_summed(): lax.all_to_all(in_blocks(value, dim, devices), axis, 0, 0, tiled=True)  45.6 us
    all_to_all x1, waiting for transfers between devices, sent_to_all(): return lax.all_to_all(copies, axis, split_axis=0, concat_axis=0, tiled=True)  31 us
    all_to_all x1, waiting for transfers between devices, on_device(): lax.all_to_all(buffer, 'expert', split_axis=0, concat_axis=1, tiled=True)  25.7 us
    all_gather x1, blocking collectives, in_one_piece(): lax.all_gather(both, axis, axis=dim, tiled=True)  17.1 us
    all_to_all x1, starting transfers between devices, on_device(): lax.all_to_all(buffer, 'expert', split_axis=0, concat_axis=1, tiled=True)  10.3 us
    all_to_all x1, starting transfers between devices, sent_to_all(): return lax.all_to_all(copies, axis, split_axis=0, concat_axis=0, tiled=True)  7.96 us
    dot_general x2, matrix products, newton_rows(): jnp.einsum('eirk,eikc->eirc', left_product, whole_now, precision=lax.Prec...  5.59 us
    dot_general x2, matrix products, newton_rows(): jnp.einsum('eirk,eikc->eirc', rows_now, matrix, precision=lax.Precision.H...  5.38 us
  transfers between devices with their start and end apart: 2, of which 2 were waited for; matrix products, arithmetic and copies ran while one was open for 0% of the time, Pallas kernels for 0%

commit v1 on v0

v1 whole, which is shorter than its diff:
```python
import jax
import jax.numpy as jnp
from jax import lax
from jax.experimental import pallas as pl
from jax.experimental.pallas import tpu as pltpu
from jax.sharding import PartitionSpec as P

MESH = pl.DeviceIdType.MESH
BLOCK = 512
HALF = 256
TOKENS_HERE = 128
LOAD_INVERSE = 1.0 / 16384.0
F32 = jnp.float32
BF16 = jnp.bfloat16


def device_at(x, y, z, c):
    return {"expert": lax.rem(z, 4) * 2 + c, "dp": x * 16 + y * 2 + z // 4}


def split_dot(rows, high, low):
    top = rows.astype(BF16)
    rest = (rows - top.astype(F32)).astype(BF16)
    both = jnp.concatenate([top, rest], axis=0)
    first = jnp.dot(both, high, preferred_element_type=F32)
    second = jnp.dot(top, low, preferred_element_type=F32)
    count = rows.shape[0]
    return first[:count] + (first[count:] + second)


def refresh(
    feat, grad, route, share, mask, damp, out,
    tok, wts, other, other_w, spread, gram, packed, diag_out, parts, diag_parts,
    total, diag_total, high, low, rows_out,
    tok_send, tok_recv, wts_send, wts_recv, fwd_send, fwd_wsend,
    part_send, part_recv, diag_send, diag_recv, diag_back_send, diag_back_recv,
    share_send, share_recv, share_fwd, out_send, out_recv, out_fwd,
):
    expert_at, dp_at = lax.axis_index("expert"), lax.axis_index("dp")
    c, zl = lax.rem(expert_at, 2), expert_at // 2
    zh, y, x = lax.rem(dp_at, 2), lax.rem(dp_at // 2, 8), dp_at // 16
    z = zh * 4 + zl
    j, b = z // 2, lax.rem(z, 2)
    sib = 1 - c
    parity = lax.rem(x, 2)
    mate = x + 1 - 2 * parity
    cross = 3 - x
    slot_me = (y * 2 + b) * 2 + c
    source_me = y * 8 + z
    sums_diag = (y == 0) & (b == 0) & (c == 0)
    own_part = c == lax.rem(j, 2)

    def remote(src, dst, send, recv, where):
        return pltpu.make_async_remote_copy(
            src_ref=src, dst_ref=dst, send_sem=send, recv_sem=recv,
            device_id=where, device_id_type=MESH,
        )

    barrier = pltpu.get_barrier_semaphore()

    def greet(where):
        pl.semaphore_signal(barrier, inc=1, device_id=where, device_id_type=MESH)

    greet(device_at(mate, y, z, c))
    greet(device_at(cross, y, z, c))

    def greet_part(i, _):
        @pl.when(jnp.logical_not(own_part & (i == source_me)))
        def _():
            greet(device_at(x, i // 8, lax.rem(i, 8), lax.rem(j, 2)))
        return 0
    lax.fori_loop(0, 64, greet_part, 0)

    def greet_block(i, _):
        k = lax.rem(slot_me + i, 32)
        greet(device_at(x, k // 4, 2 * j + lax.rem(k // 2, 2), lax.rem(k, 2)))
        return 0
    lax.fori_loop(1, 32, greet_block, 0)

    out_self = (c == x // 2) & (b == zh) & (lax.rem(j, 2) == c)

    def greet_out(i, _):
        f, e = i // 4, 2 * lax.rem(i, 4) + c
        xs, js = 2 * f + e // 4, lax.rem(e, 4)
        @pl.when(jnp.logical_not(out_self & (xs == x) & (js == j)))
        def _():
            greet(device_at(xs, y, 2 * js + zh, x // 2))
        return 0
    lax.fori_loop(0, 8, greet_out, 0)

    lanes = lax.broadcasted_iota(jnp.int32, (8, TOKENS_HERE), 0)
    keep = jnp.broadcast_to(mask[...].astype(F32), (8, TOKENS_HERE))
    is_first = route[0:1, :] == lanes
    is_second = route[1:2, :] == lanes
    share_b = jnp.broadcast_to(share[...], (8, TOKENS_HERE))
    weight_act = jnp.where(is_first | is_second, keep, 0.0)
    weight_grad = jnp.where(is_first, share_b * keep, jnp.where(is_second, (1.0 - share_b) * keep, 0.0))

    @pl.when(x < 2)
    def _():
        tok[0] = feat[...]
        other[...] = grad[...]
        wts[0] = weight_act
        other_w[...] = weight_grad

    @pl.when(x >= 2)
    def _():
        tok[0] = grad[...]
        other[...] = feat[...]
        wts[0] = weight_grad
        other_w[...] = weight_act

    waiting = (
        2 + 64 - own_part.astype(jnp.int32) + 31 + 8 - out_self.astype(jnp.int32)
    )
    pl.semaphore_wait(barrier, waiting)

    to_cross = remote(other, tok.at[1], tok_send.at[0], tok_recv.at[1], device_at(cross, y, z, c))
    to_cross_w = remote(other_w, wts.at[1], wts_send.at[0], wts_recv.at[1], device_at(cross, y, z, c))
    to_mate = remote(tok.at[0], tok.at[2], tok_send.at[1], tok_recv.at[2], device_at(mate, y, z, c))
    to_mate_w = remote(wts.at[0], wts.at[2], wts_send.at[1], wts_recv.at[2], device_at(mate, y, z, c))
    on_mate = remote(tok.at[1], tok.at[3], tok_send.at[2], tok_recv.at[3], device_at(mate, y, z, c))
    on_mate_w = remote(wts.at[1], wts.at[3], wts_send.at[2], wts_recv.at[3], device_at(mate, y, z, c))

    def to_sib(i):
        where = device_at(x, y, z, sib)
        return (
            remote(tok.at[i], tok.at[4 + i], fwd_send.at[i], tok_recv.at[4 + i], where),
            remote(wts.at[i], wts.at[4 + i], fwd_wsend.at[i], wts_recv.at[4 + i], where),
        )

    def from_sib(i):
        for copy in to_sib(i):
            copy.wait_recv()

    def started(copies):
        for copy in copies:
            copy.start()

    def landed(copies):
        for copy in copies:
            copy.wait_recv()

    def gather_gram(i, begin):
        for kk in range(2):
            e = 4 * parity + 2 * kk + c
            for h, slot in enumerate((i, 4 + i)):
                row = wts[slot, pl.ds(e, 1), :]
                column = jnp.transpose(jnp.broadcast_to(row, (TOKENS_HERE, TOKENS_HERE)))
                for q in range(4):
                    piece = tok[slot, :, 128 * q : 128 * q + 128].astype(F32) * column
                    spread[kk, 128 * h : 128 * h + 128, 128 * q : 128 * q + 128] = piece.astype(BF16)
            left, right = spread[kk, :, :HALF], spread[kk, :, HALF:]
            for n, (one, two) in enumerate(((left, right), (left, left), (right, right))):
                term = lax.dot_general(one, two, (((0,), (0,)), ((), ())), preferred_element_type=F32)
                gram[kk, n] = term if begin else gram[kk, n] + term

    started((to_cross_w, to_cross, to_mate_w, to_mate))
    started(to_sib(0))
    from_sib(0)
    gather_gram(0, True)
    landed((to_cross_w, to_cross))
    started((on_mate_w, on_mate))
    started(to_sib(1))
    landed((to_mate_w, to_mate))
    started(to_sib(2))
    from_sib(1)
    gather_gram(1, False)
    landed((on_mate_w, on_mate))
    started(to_sib(3))
    from_sib(2)
    gather_gram(2, False)
    from_sib(3)
    gather_gram(3, False)

    r_half = lax.broadcasted_iota(jnp.int32, (HALF, HALF), 0)
    c_half = lax.broadcasted_iota(jnp.int32, (HALF, HALF), 1)
    damp_row = jnp.where(x < 2, damp[0:1, :], damp[1:2, :])
    for kk in range(2):
        upper, lower = gram[kk, 1], gram[kk, 2]
        packed[kk, 0:16] = gram[kk, 0].astype(BF16).reshape(16, 16, HALF)
        packed[kk, 16:32] = jnp.where(r_half <= c_half, upper, lower).astype(BF16).reshape(16, 16, HALF)
        on_diag = r_half == c_half
        d_up = jnp.sum(jnp.where(on_diag, upper, 0.0), axis=0, keepdims=True)
        d_low = jnp.sum(jnp.where(on_diag, lower, 0.0), axis=0, keepdims=True)
        mine = (expert_at == 4 * parity + 2 * kk + c) & (y == 0) & (zh == 0)
        diag_out[kk, 0:1] = d_up[:, :128]
        diag_out[kk, 1:2] = d_up[:, 128:]
        diag_out[kk, 2:3] = d_low[:, :128]
        diag_out[kk, 3:4] = d_low[:, 128:]
        diag_out[kk, 4:8] = jnp.broadcast_to(jnp.where(mine, damp_row, 0.0), (4, 128))

    def part_copy(kk, k):
        jj = 2 * kk + c
        where = device_at(x, k // 4, 2 * jj + lax.rem(k // 2, 2), lax.rem(k, 2))
        return remote(packed.at[kk, k], parts.at[source_me], part_send.at[kk, k], part_recv, where)

    def is_me(kk, k):
        return own_part & (2 * kk + c == j) & (k == slot_me)

    for kk in range(2):
        jj = 2 * kk + c
        there = (y == 0) & (c == 0) & (z == 2 * jj)
        diag_copy = remote(
            diag_out.at[kk], diag_parts.at[source_me], diag_send.at[kk], diag_recv,
            device_at(x, 0, 2 * jj, 0),
        )

        @pl.when(jnp.logical_not(there))
        def _():
            diag_copy.start()

        @pl.when(there)
        def _():
            pltpu.make_async_copy(diag_out.at[kk], diag_parts.at[source_me], diag_recv).start()

        def send_part(i, _):
            k = lax.rem(slot_me + i, 32)

            @pl.when(jnp.logical_not(is_me(kk, k)))
            def _():
                part_copy(kk, k).start()

            @pl.when(is_me(kk, k))
            def _():
                pltpu.make_async_copy(packed.at[kk, k], parts.at[source_me], part_recv).start()
            return 0
        lax.fori_loop(0, 32, send_part, 0)

    pltpu.make_async_copy(parts, parts, part_recv).wait()
    summed = parts[0].astype(F32)
    for i in range(1, 64):
        summed = summed + parts[i].astype(F32)
    total[slot_me] = summed

    def share_copy(i):
        k = lax.rem(slot_me + 2 * i, 32)
        where = device_at(x, k // 4, 2 * j + lax.rem(k // 2, 2), c)
        return remote(total.at[slot_me], total.at[slot_me], share_send.at[i], share_recv.at[slot_me], where)

    def share_on(k):
        return remote(
            total.at[k], total.at[k], share_fwd.at[k // 2], share_recv.at[k], device_at(x, y, z, sib)
        )

    def send_share(i, _):
        share_copy(i).start()
        return 0
    lax.fori_loop(1, 16, send_share, 0)
    share_on(slot_me).start()

    def diag_back(k):
        where = device_at(x, k // 4, 2 * j + lax.rem(k // 2, 2), lax.rem(k, 2))
        return remote(diag_total, diag_total, diag_back_send.at[k], diag_back_recv, where)

    @pl.when(sums_diag)
    def _():
        pltpu.make_async_copy(diag_parts, diag_parts, diag_recv).wait()
        diag_total[...] = jnp.sum(diag_parts[...], axis=0)

        def send_diag(k, _):
            diag_back(k).start()
            return 0
        lax.fori_loop(1, 32, send_diag, 0)

    def pass_on(i, _):
        k = lax.rem(slot_me + 32 - 2 * i, 32)
        share_on(k).wait_recv()
        share_on(k).start()
        return 0
    lax.fori_loop(1, 16, pass_on, 0)

    def from_other(i, _):
        share_on(2 * i + sib).wait_recv()
        return 0
    lax.fori_loop(0, 16, from_other, 0)

    @pl.when(jnp.logical_not(sums_diag))
    def _():
        diag_back(0).wait_recv()

    corner = total[0:16].reshape(HALF, HALF) * LOAD_INVERSE
    folded = total[16:32].reshape(HALF, HALF) * LOAD_INVERSE
    turned = jnp.transpose(folded)
    damping = diag_total[4:5, :]
    d_up = jnp.concatenate(
        [diag_total[0:1] * LOAD_INVERSE + damping, diag_total[1:2] * LOAD_INVERSE + damping], axis=1
    )
    d_low = jnp.concatenate(
        [diag_total[2:3] * LOAD_INVERSE + damping, diag_total[3:4] * LOAD_INVERSE + damping], axis=1
    )
    upper = jnp.where(r_half < c_half, folded, jnp.where(r_half > c_half, turned, d_up))
    lower = jnp.where(r_half > c_half, folded, jnp.where(r_half < c_half, turned, d_low))
    corner_turned = jnp.transpose(corner)
    sums_left = jnp.sum(jnp.abs(upper) + jnp.abs(corner_turned), axis=0, keepdims=True)
    sums_right = jnp.sum(jnp.abs(corner) + jnp.abs(lower), axis=0, keepdims=True)
    largest = jnp.max(jnp.maximum(sums_left, sums_right), axis=1, keepdims=True)
    scale = 1.0 / largest
    one = jnp.where(r_half == c_half, 1.0, 0.0)
    for block, at in (
        (one - scale * upper, (slice(0, HALF), slice(0, HALF))),
        (-scale * corner, (slice(0, HALF), slice(HALF, BLOCK))),
        (-scale * corner_turned, (slice(HALF, BLOCK), slice(0, HALF))),
        (one - scale * lower, (slice(HALF, BLOCK), slice(HALF, BLOCK))),
    ):
        top = block.astype(BF16)
        high[at] = top
        low[at] = (block - top.astype(F32)).astype(BF16)

    row_at = lax.broadcasted_iota(jnp.int32, (16, BLOCK), 0)
    col_at = lax.broadcasted_iota(jnp.int32, (16, BLOCK), 1)
    wanted = 8 * (16 * (2 * c + row_at // 8) + 2 * y + b) + lax.rem(row_at, 8)
    unit = jnp.where(col_at == wanted, 1.0, 0.0)
    lead = unit
    for _ in range(7):
        lead = unit + split_dot(lead, high[...], low[...])
    result = lead * scale
    rows_out[0] = result[:8]
    rows_out[1] = result[8:]

    f_me, e_me = x // 2, 4 * parity + j
    core_there = lax.rem(j, 2)

    def out_copy(n):
        i, zt = n // 4, 4 * b + lax.rem(n, 4)
        return remote(
            rows_out.at[i], out.at[f_me, e_me], out_send.at[n], out_recv.at[f_me * 8 + e_me],
            device_at(2 * c + i, y, zt, core_there),
        )

    def out_here(n):
        return (2 * c + n // 4 == x) & (4 * b + lax.rem(n, 4) == z) & (core_there == c)

    def send_out(n, _):
        @pl.when(jnp.logical_not(out_here(n)))
        def _():
            out_copy(n).start()

        @pl.when(out_here(n))
        def _():
            pltpu.make_async_copy(
                rows_out.at[n // 4], out.at[f_me, e_me], out_recv.at[f_me * 8 + e_me]
            ).start()
        return 0
    lax.fori_loop(0, 8, send_out, 0)

    def out_on(f, e):
        return remote(
            out.at[f, e], out.at[f, e], out_fwd.at[f * 4 + e // 2], out_recv.at[f * 8 + e],
            device_at(x, y, z, sib),
        )

    def pass_out(n, _):
        copy = out_on(n // 4, 2 * lax.rem(n, 4) + c)
        copy.wait_recv()
        copy.start()
        return 0
    lax.fori_loop(0, 8, pass_out, 0)

    def take_out(n, _):
        out_on(n // 4, 2 * lax.rem(n, 4) + sib).wait_recv()
        return 0
    lax.fori_loop(0, 8, take_out, 0)

    for copy in (to_cross, to_cross_w, to_mate, to_mate_w, on_mate, on_mate_w):
        copy.wait_send()
    for i in range(4):
        for copy in to_sib(i):
            copy.wait_send()
    for kk in range(2):
        jj = 2 * kk + c

        @pl.when(jnp.logical_not((y == 0) & (c == 0) & (z == 2 * jj)))
        def _():
            remote(
                diag_out.at[kk], diag_parts.at[source_me], diag_send.at[kk], diag_recv,
                device_at(x, 0, 2 * jj, 0),
            ).wait_send()

        def part_left(k, _):
            @pl.when(jnp.logical_not(is_me(kk, k)))
            def _():
                part_copy(kk, k).wait_send()
            return 0
        lax.fori_loop(0, 32, part_left, 0)

    def share_left(i, _):
        share_copy(i).wait_send()
        return 0
    lax.fori_loop(1, 16, share_left, 0)

    def share_on_left(i, _):
        share_on(2 * i + c).wait_send()
        return 0
    lax.fori_loop(0, 16, share_on_left, 0)

    @pl.when(sums_diag)
    def _():
        def diag_left(k, _):
            diag_back(k).wait_send()
            return 0
        lax.fori_loop(1, 32, diag_left, 0)

    def out_left(n, _):
        @pl.when(jnp.logical_not(out_here(n)))
        def _():
            out_copy(n).wait_send()
        return 0
    lax.fori_loop(0, 8, out_left, 0)

    def out_on_left(n, _):
        out_on(n // 4, 2 * lax.rem(n, 4) + c).wait_send()
        return 0
    lax.fori_loop(0, 8, out_on_left, 0)


def on_device(features, gradients, route_ids, gate_share, token_mask, damping):
    route = route_ids.T
    share = gate_share.reshape(1, TOKENS_HERE)
    mask = token_mask.reshape(1, TOKENS_HERE)
    damp = jnp.broadcast_to(damping.reshape(2, 1), (2, 128))
    dma = pltpu.SemaphoreType.DMA
    out = pl.pallas_call(
        refresh,
        out_shape=jax.ShapeDtypeStruct((2, 8, 8, BLOCK), F32),
        in_specs=[pl.BlockSpec(memory_space=pltpu.VMEM)] * 6,
        out_specs=pl.BlockSpec(memory_space=pltpu.VMEM),
        scratch_shapes=[
            pltpu.VMEM((8, TOKENS_HERE, BLOCK), BF16),
            pltpu.VMEM((8, 8, TOKENS_HERE), F32),
            pltpu.VMEM((TOKENS_HERE, BLOCK), BF16),
            pltpu.VMEM((8, TOKENS_HERE), F32),
            pltpu.VMEM((2, 2 * TOKENS_HERE, BLOCK), BF16),
            pltpu.VMEM((2, 3, HALF, HALF), F32),
            pltpu.VMEM((2, 32, 16, HALF), BF16),
            pltpu.VMEM((2, 8, 128), F32),
            pltpu.VMEM((64, 16, HALF), BF16),
            pltpu.VMEM((64, 8, 128), F32),
            pltpu.VMEM((32, 16, HALF), F32),
            pltpu.VMEM((8, 128), F32),
            pltpu.VMEM((BLOCK, BLOCK), BF16),
            pltpu.VMEM((BLOCK, BLOCK), BF16),
            pltpu.VMEM((2, 8, BLOCK), F32),
            dma((3,)), dma((8,)), dma((3,)), dma((8,)), dma((4,)), dma((4,)),
            dma((2, 32)), dma, dma((2,)), dma, dma((32,)), dma,
            dma((16,)), dma((32,)), dma((16,)), dma((8,)), dma((16,)), dma((8,)),
        ],
        compiler_params=pltpu.CompilerParams(
            collective_id=0, has_side_effects=True, vmem_limit_bytes=40 * 1024 * 1024
        ),
    )(features, gradients, route, share, mask, damp)
    return out[0].reshape(8, 1, 8, BLOCK), out[1].reshape(8, 1, 8, BLOCK)


def solution(mesh):
    placed = (
        P(("expert", "dp"), None),
        P(("expert", "dp"), None),
        P(("expert", "dp"), None),
        P(("expert", "dp")),
        P(("expert", "dp")),
        P("expert", None, None),
    )
    return jax.shard_map(
        on_device,
        mesh=mesh,
        in_specs=placed,
        out_specs=(P(None, None, "dp", None), P(None, None, "dp", None)),
        check_vma=False,
    )
```

time: 181 us -> 76.4 us (0.42)
  Pallas kernels: 0 us -> 71.7 us
  blocking collectives: 62.7 us -> 0 us
  waiting for transfers between devices: 56.8 us -> 0 us
  starting transfers between devices: 18.3 us -> 0 us
  local copies, waits for them, and re-layouts: 18.5 us -> 3.84 us
  other arithmetic: 11.9 us -> 0 us
  matrix products: 11.7 us -> 0 us
    pallas_call x0 -> x1, Pallas kernels: none -> 71.7 us  [on_device(): pl.pallas_call(refresh, out_shape=jax.ShapeDtypeStruct((2, 8, 8, BLOCK),...]
    all_to_all x2 -> x0, waiting for transfers between devices: 56.8 us -> none  [the longest x1 31 us: sent_to_all(): return lax.all_to_all(copies, axis, split_axis=0, concat_axis=0, tiled=True)]
    all_to_all x1 -> x0, blocking collectives: 45.6 us -> none  [sent_and_summed(): lax.all_to_all(in_blocks(value, dim, devices), axis, 0, 0, tiled=True)]
    all_to_all x2 -> x0, starting transfers between devices: 18.3 us -> none  [the longest x1 10.3 us: on_device(): lax.all_to_all(buffer, 'expert', split_axis=0, concat_axis=1, tiled=True)]
    all_gather x1 -> x0, blocking collectives: 17.1 us -> none  [in_one_piece(): lax.all_gather(both, axis, axis=dim, tiled=True)]
    dot_general x5 -> x0, matrix products: 11.7 us -> none  [the longest x2 5.59 us: newton_rows(): jnp.einsum('eirk,eikc->eirc', left_product, whole_now, precision=lax.Prec...]
    gather x2 -> x0, local copies, waits for them, and re-layouts: 2.85 us -> none  [on_device(): jnp.take(padded, slot_table(route_ids, capacity), axis=0)]
    select_n x5 -> x0, other arithmetic: 2.67 us -> none  [the longest x1 1.21 us: fold_unpack(): upper_left = jnp.where(row_ids <= col_ids, head, jnp.swapaxes(head, 2, 3))]
  transfers between devices with their start and end apart: 2 -> 0, of which waited for: 2 -> 0; matrix products, arithmetic and copies ran while one was open for 0% -> 0% of each run, Pallas kernels for 0% -> 0%
where the time goes in v1:
time: 76.4 us; the launch traced here: 76.2 us
  Pallas kernels  71.7 us (94%)
  local copies, waits for them, and re-layouts  3.84 us (5%)
    pallas_call x1, Pallas kernels, on_device(): pl.pallas_call(refresh, out_shape=jax.ShapeDtypeStruct((2, 8, 8, BLOCK),...  71.7 us
    unnamed x13, local copies, waits for them, and re-layouts  3.77 us

profile of v1, /device:TPU:1, one launch (start us, length us, event | category | flops | bytes accessed | tf_op | source)
XLA Modules:
  0.0 76.2 jit_solution(4998095345090249067)
XLA Ops:
  0.6 0.0 copy-start.5
  0.6 0.0 copy-start.4
  0.7 0.6 copy-done.5
  1.3 0.0 copy-start.2
  1.3 0.0 copy-start.3
  1.3 0.1 broadcast_in_dim.8.damp
  1.4 0.0 copy-done.4
  1.4 0.6 copy-done.2
  2.0 0.0 copy-done.3
  2.0 0.0 copy-start
  2.0 0.9 %copy-done = bf16[128,512]{1,0:T(8,128)(2,1)S(1)} copy-done((bf16[128,512]{1,0:T(8,128)(2,1)S(1)}, bf16[128,512]{1,0:T(8,128)(2,1)}, u32[]{:S(2)}) %copy-start) | copy-done | bytes 131096
  2.9 0.0 copy-start.1
  2.9 0.9 %copy-done.1 = bf16[128,512]{1,0:T(8,128)(2,1)S(1)} copy-done((bf16[128,512]{1,0:T(8,128)(2,1)S(1)}, bf16[128,512]{1,0:T(8,128)(2,1)}, u32[]{:S(2)}) %copy-start.1) | copy-done | bytes 131096
  3.8 71.7 %shard_map.77 = f32[2,8,8,512]{3,2,1,0:T(8,128)S(1)} custom-call(bf16[128,512]{1,0:T(8,128)(2,1)S(1)} %copy-done, bf16[128,512]{1,0:T(8,128)(2,1)S(1)} %copy-done.1, s32[2,128]{1,0:T(2,128)S(1)} %bitcast.12, f32[1,128]{1,0:T(1,128)S(1)} %bitcast.13, s32[1,128]{1,0:T(1,128)S(1)} %bitcast.14, f32[2,128]{1,0:T(2,128)S(1)} %broadcast_in_dim.8.damp), custom_call_target="tpu_custom_call" | custom-call | tf_op jit(solution)/shard_map/pallas_call | solution.py:423
  75.5 0.7 slice_bitcast_fusion
Async XLA Ops:
  0.6 0.7 copy-start.5
  0.6 0.7 copy-start.4
  1.3 0.7 copy-start.2
  1.3 0.7 copy-start.3
  2.0 0.9 %copy-start = (bf16[128,512]{1,0:T(8,128)(2,1)S(1)}, bf16[128,512]{1,0:T(8,128)(2,1)}, u32[]{:S(2)}) copy-start(bf16[128,512]{1,0:T(8,128)(2,1)} %feat.1) | copy-start | bytes 393220
  2.9 0.9 %copy-start.1 = (bf16[128,512]{1,0:T(8,128)(2,1)S(1)}, bf16[128,512]{1,0:T(8,128)(2,1)}, u32[]{:S(2)}) copy-start(bf16[128,512]{1,0:T(8,128)(2,1)} %grad.1) | copy-start | bytes 393220

commit v2 on v1

v2 whole, which is shorter than its diff:
```python
import jax
import jax.numpy as jnp
from jax import lax
from jax.experimental import pallas as pl
from jax.experimental.pallas import tpu as pltpu
from jax.sharding import PartitionSpec as P

MESH = pl.DeviceIdType.MESH
BLOCK = 512
HALF = 256
TOKENS_HERE = 128
LOAD_INVERSE = 1.0 / 16384.0
F32 = jnp.float32
BF16 = jnp.bfloat16


def device_at(x, y, z, c):
    return {"expert": lax.rem(z, 4) * 2 + c, "dp": x * 16 + y * 2 + lax.div(z, 4)}


def split_dot(rows, high, low):
    top = rows.astype(BF16)
    rest = (rows - top.astype(F32)).astype(BF16)
    both = jnp.concatenate([top, rest], axis=0)
    first = jnp.dot(both, high, preferred_element_type=F32)
    second = jnp.dot(top, low, preferred_element_type=F32)
    count = rows.shape[0]
    return first[:count] + (first[count:] + second)


def refresh(
    feat, grad, route_in, share_in, mask_in, damp_in, out,
    route, share, mask, damp,
    tok, wts, other, other_w, spread, gram, corners, folds, diag_out,
    by_z, by_y, z_sums, y_sums, last, diag_parts,
    total, diag_total, high, low, rows_out,
    load_sem, tok_send, tok_recv, wts_send, wts_recv, fwd_send, fwd_wsend, both_in,
    z_send, z_recv, y_send, y_recv, z2_send, y2_send, last_recv,
    diag_send, diag_recv, diag_back_send, diag_back_recv,
    share_send, share_recv, share_fwd, out_send, out_recv, out_fwd,
):
    expert_at, dp_at = lax.axis_index("expert"), lax.axis_index("dp")
    c, zl = lax.rem(expert_at, 2), lax.div(expert_at, 2)
    zh, y, x = lax.rem(dp_at, 2), lax.rem(lax.div(dp_at, 2), 8), lax.div(dp_at, 16)
    z = zh * 4 + zl
    j, b = lax.div(z, 2), lax.rem(z, 2)
    sib = 1 - c
    parity, half_x = lax.rem(x, 2), lax.div(x, 2)
    mate = x + 1 - 2 * parity
    cross = 3 - x
    row_me = jnp.where(c == 0, b * 8 + y, y * 2 + b)
    chip_me = y * 2 + b
    sums_diag = (y == 0) & (b == 0) & (c == 0)
    sums_z = c == lax.rem(j, 2)
    sibling = {"expert": expert_at + 1 - 2 * c, "dp": dp_at}

    def remote(src, dst, send, recv, where):
        return pltpu.make_async_remote_copy(
            src_ref=src, dst_ref=dst, send_sem=send, recv_sem=recv,
            device_id=where, device_id_type=MESH,
        )

    loads = (
        (route_in, route), (share_in, share), (mask_in, mask), (damp_in, damp),
    )
    for n, (src, dst) in enumerate(loads):
        pltpu.make_async_copy(src, dst, load_sem.at[n]).start()

    @pl.when(x < 2)
    def _():
        pltpu.make_async_copy(feat, tok.at[0], load_sem.at[4]).start()
        pltpu.make_async_copy(grad, other, load_sem.at[5]).start()

    @pl.when(x >= 2)
    def _():
        pltpu.make_async_copy(grad, tok.at[0], load_sem.at[4]).start()
        pltpu.make_async_copy(feat, other, load_sem.at[5]).start()

    barrier = pltpu.get_barrier_semaphore()

    def greet(where):
        pl.semaphore_signal(barrier, inc=1, device_id=where, device_id_type=MESH)

    greet(device_at(mate, y, z, c))
    greet(device_at(cross, y, z, c))
    greet(sibling)
    for n in range(1, 8):
        greet({"expert": expert_at, "dp": x * 16 + lax.rem(y + n, 8) * 2 + zh})
        greet(device_at(x, y, lax.rem(z + n, 8), c))

    for n, (src, dst) in enumerate(loads):
        pltpu.make_async_copy(src, dst, load_sem.at[n]).wait()
    lanes = lax.broadcasted_iota(jnp.int32, (8, TOKENS_HERE), 0)
    keep = jnp.broadcast_to(mask[...].astype(F32), (8, TOKENS_HERE))
    is_first = route[0:1, :] == lanes
    is_second = route[1:2, :] == lanes
    share_b = jnp.broadcast_to(share[...], (8, TOKENS_HERE))
    weight_act = jnp.where(is_first | is_second, keep, 0.0)
    weight_grad = jnp.where(is_first, share_b * keep, jnp.where(is_second, (1.0 - share_b) * keep, 0.0))

    @pl.when(x < 2)
    def _():
        wts[0] = weight_act
        other_w[...] = weight_grad

    @pl.when(x >= 2)
    def _():
        wts[0] = weight_grad
        other_w[...] = weight_act

    pltpu.make_async_copy(feat, tok.at[0], load_sem.at[4]).wait()
    pltpu.make_async_copy(grad, other, load_sem.at[5]).wait()
    pl.semaphore_wait(barrier, 17)
    pl.semaphore_signal(both_in, inc=1, device_id=sibling, device_id_type=MESH)

    to_cross = remote(other, tok.at[1], tok_send.at[0], tok_recv.at[1], device_at(cross, y, z, c))
    to_cross_w = remote(other_w, wts.at[1], wts_send.at[0], wts_recv.at[1], device_at(cross, y, z, c))
    to_mate = remote(tok.at[0], tok.at[2], tok_send.at[1], tok_recv.at[2], device_at(mate, y, z, c))
    to_mate_w = remote(wts.at[0], wts.at[2], wts_send.at[1], wts_recv.at[2], device_at(mate, y, z, c))
    on_mate = remote(tok.at[1], tok.at[3], tok_send.at[2], tok_recv.at[3], device_at(mate, y, z, c))
    on_mate_w = remote(wts.at[1], wts.at[3], wts_send.at[2], wts_recv.at[3], device_at(mate, y, z, c))

    def to_sib(i):
        where = sibling
        return (
            remote(tok.at[i], tok.at[4 + i], fwd_send.at[i], tok_recv.at[4 + i], where),
            remote(wts.at[i], wts.at[4 + i], fwd_wsend.at[i], wts_recv.at[4 + i], where),
        )

    def from_sib(i):
        for copy in to_sib(i):
            copy.wait_recv()

    def started(copies):
        for copy in copies:
            copy.start()

    def landed(copies):
        for copy in copies:
            copy.wait_recv()

    def gather_gram(i, begin):
        for kk in range(2):
            e = 4 * parity + 2 * kk + c
            for h, slot in enumerate((i, 4 + i)):
                row = wts[slot, pl.ds(e, 1), :]
                column = jnp.transpose(jnp.broadcast_to(row, (TOKENS_HERE, TOKENS_HERE)))
                for q in range(4):
                    piece = tok[slot, :, 128 * q : 128 * q + 128].astype(F32) * column
                    spread[kk, 128 * h : 128 * h + 128, 128 * q : 128 * q + 128] = piece.astype(BF16)
            left, right = spread[kk, :, :HALF], spread[kk, :, HALF:]
            for n, (one, two) in enumerate(((left, right), (left, left), (right, right))):
                term = lax.dot_general(one, two, (((0,), (0,)), ((), ())), preferred_element_type=F32)
                gram[kk, n] = term if begin else gram[kk, n] + term

    started((to_cross_w, to_cross, to_mate_w, to_mate))
    started(to_sib(0))
    from_sib(0)
    gather_gram(0, True)
    landed((to_cross_w, to_cross))
    started((on_mate_w, on_mate))
    started(to_sib(1))
    landed((to_mate_w, to_mate))
    started(to_sib(2))
    from_sib(1)
    gather_gram(1, False)
    landed((on_mate_w, on_mate))
    started(to_sib(3))
    from_sib(2)
    gather_gram(2, False)
    from_sib(3)
    gather_gram(3, False)

    pl.semaphore_wait(both_in, 1)

    def z_copy(kk, bb):
        return remote(
            corners.at[kk, pl.ds(8 * bb, 8)], by_z.at[z], z_send.at[kk, bb], z_recv.at[z],
            device_at(x, y, 4 * kk + 2 * c + bb, c),
        )

    def z_self(kk, bb):
        return z == 4 * kk + 2 * c + bb

    def y_copy(n):
        there = lax.rem(y + n, 8)
        return remote(
            folds.at[there], by_y.at[y], y_send.at[n], y_recv.at[y],
            {"expert": expert_at, "dp": x * 16 + there * 2 + zh},
        )

    def own_z():
        return pltpu.make_async_copy(corners.at[lax.div(z, 4), pl.ds(8 * b, 8)], by_z.at[z], z_recv.at[z])

    def own_y():
        return pltpu.make_async_copy(folds.at[y], by_y.at[y], y_recv.at[y])

    r_half = lax.broadcasted_iota(jnp.int32, (HALF, HALF), 0)
    c_half = lax.broadcasted_iota(jnp.int32, (HALF, HALF), 1)
    on_diag = r_half == c_half
    for kk in range(2):
        corners[kk] = gram[kk, 0].astype(BF16).reshape(16, 16, HALF)
        for bb in range(2):
            @pl.when(jnp.logical_not(z_self(kk, bb)))
            def _():
                z_copy(kk, bb).start()
    for kk in range(2):
        upper, lower = gram[kk, 1], gram[kk, 2]
        folded = jnp.where(r_half <= c_half, upper, lower).astype(BF16)
        folds[:, kk] = folded.reshape(8, 2, 16, HALF)
    for n in range(1, 8):
        y_copy(n).start()
    own_y().start()

    @pl.when(sums_z)
    def _():
        own_z().start()

    damp_row = jnp.where(x < 2, damp[0:1, :], damp[1:2, :])
    for kk in range(2):
        upper, lower = gram[kk, 1], gram[kk, 2]
        d_up = jnp.sum(jnp.where(on_diag, upper, 0.0), axis=0, keepdims=True)
        d_low = jnp.sum(jnp.where(on_diag, lower, 0.0), axis=0, keepdims=True)
        mine = (expert_at == 4 * parity + 2 * kk + c) & (y == 0) & (zh == 0)
        diag_out[kk, 0:1] = d_up[:, :128]
        diag_out[kk, 1:2] = d_up[:, 128:]
        diag_out[kk, 2:3] = d_low[:, :128]
        diag_out[kk, 3:4] = d_low[:, 128:]
        diag_out[kk, 4:8] = jnp.broadcast_to(jnp.where(mine, damp_row, 0.0), (4, 128))

    sum_y = None
    for n in range(8):
        there = lax.rem(y + 8 - n, 8)
        pltpu.make_async_copy(folds.at[0], by_y.at[there], y_recv.at[there]).wait()
        term = by_y[there].astype(F32)
        sum_y = term if n == 0 else sum_y + term
    y_sums[...] = sum_y

    def y2_copy(kk, bb):
        return remote(
            y_sums.at[kk, bb], last.at[z], y2_send.at[kk, bb], last_recv.at[z],
            device_at(x, y, 4 * kk + 2 * c + bb, 1),
        )

    def y2_self(kk, bb):
        return (c == 1) & z_self(kk, bb)

    for kk in range(2):
        for bb in range(2):
            @pl.when(jnp.logical_not(y2_self(kk, bb)))
            def _():
                y2_copy(kk, bb).start()

            @pl.when(y2_self(kk, bb))
            def _():
                pltpu.make_async_copy(y_sums.at[kk, bb], last.at[z], last_recv.at[z]).start()

    def diag_copy(kk):
        return remote(
            diag_out.at[kk], diag_parts.at[y * 8 + z], diag_send.at[kk], diag_recv,
            device_at(x, 0, 4 * kk + 2 * c, 0),
        )

    def diag_self(kk):
        return (y == 0) & (c == 0) & (z == 4 * kk)

    for kk in range(2):
        @pl.when(jnp.logical_not(diag_self(kk)))
        def _():
            diag_copy(kk).start()

        @pl.when(diag_self(kk))
        def _():
            pltpu.make_async_copy(diag_out.at[kk], diag_parts.at[y * 8 + z], diag_recv).start()

    def z2_copy(there):
        return remote(
            z_sums.at[there], last.at[y], z2_send.at[there], last_recv.at[y],
            device_at(x, there, z, 0),
        )

    def z2_self(there):
        return (c == 0) & (there == y)

    @pl.when(sums_z)
    def _():
        sum_z = None
        for n in range(8):
            there = lax.rem(z + 8 - n, 8)
            pltpu.make_async_copy(by_z.at[there], by_z.at[there], z_recv.at[there]).wait()
            term = by_z[there].astype(F32)
            sum_z = term if n == 0 else sum_z + term
        z_sums[...] = sum_z

        def z2_start(n, _):
            there = lax.rem(y + n, 8)

            @pl.when(jnp.logical_not(z2_self(there)))
            def _():
                z2_copy(there).start()

            @pl.when(z2_self(there))
            def _():
                pltpu.make_async_copy(z_sums.at[there], last.at[y], last_recv.at[y]).start()
            return 0
        lax.fori_loop(0, 8, z2_start, 0)

    summed = None
    for n in range(8):
        pltpu.make_async_copy(last.at[n], last.at[n], last_recv.at[n]).wait()
        summed = last[n] if n == 0 else summed + last[n]
    total[c, row_me] = summed

    def row_of(core, chip):
        yy, bb = lax.div(chip, 2), lax.rem(chip, 2)
        return jnp.where(core == 0, bb * 8 + yy, yy * 2 + bb)

    def share_copy(i):
        k = lax.rem(chip_me + i, 16)
        where = device_at(x, lax.div(k, 2), 2 * j + lax.rem(k, 2), c)
        own = total.at[c, row_me]
        return remote(own, own, share_send.at[i], share_recv.at[c, row_me], where)

    def share_on(row):
        one = total.at[c, row]
        return remote(one, one, share_fwd.at[row], share_recv.at[c, row], sibling)

    def send_share(i, _):
        share_copy(i).start()
        return 0
    lax.fori_loop(1, 16, send_share, 0)
    share_on(row_me).start()

    def diag_back(k):
        where = device_at(x, lax.div(k, 4), 2 * j + lax.rem(lax.div(k, 2), 2), lax.rem(k, 2))
        return remote(diag_total, diag_total, diag_back_send.at[k], diag_back_recv, where)

    @pl.when(sums_diag)
    def _():
        pltpu.make_async_copy(diag_parts, diag_parts, diag_recv).wait()
        diag_total[...] = jnp.sum(diag_parts[...], axis=0)

        def send_diag(k, _):
            diag_back(k).start()
            return 0
        lax.fori_loop(1, 32, send_diag, 0)

    def pass_on(i, _):
        row = row_of(c, lax.rem(chip_me + 16 - i, 16))
        share_on(row).wait_recv()
        share_on(row).start()
        return 0
    lax.fori_loop(1, 16, pass_on, 0)

    def from_other(row, _):
        one = total.at[sib, row]
        remote(one, one, share_fwd.at[row], share_recv.at[sib, row], sibling).wait_recv()
        return 0
    lax.fori_loop(0, 16, from_other, 0)

    @pl.when(jnp.logical_not(sums_diag))
    def _():
        diag_back(0).wait_recv()

    corner = total[0].reshape(HALF, HALF) * LOAD_INVERSE
    folded = total[1].reshape(HALF, HALF) * LOAD_INVERSE
    turned = jnp.transpose(folded)
    damping = diag_total[4:5, :]
    d_up = jnp.concatenate(
        [diag_total[0:1] * LOAD_INVERSE + damping, diag_total[1:2] * LOAD_INVERSE + damping], axis=1
    )
    d_low = jnp.concatenate(
        [diag_total[2:3] * LOAD_INVERSE + damping, diag_total[3:4] * LOAD_INVERSE + damping], axis=1
    )
    upper = jnp.where(r_half < c_half, folded, jnp.where(r_half > c_half, turned, d_up))
    lower = jnp.where(r_half > c_half, folded, jnp.where(r_half < c_half, turned, d_low))
    corner_turned = jnp.transpose(corner)
    sums_left = jnp.sum(jnp.abs(upper) + jnp.abs(corner_turned), axis=0, keepdims=True)
    sums_right = jnp.sum(jnp.abs(corner) + jnp.abs(lower), axis=0, keepdims=True)
    largest = jnp.max(jnp.maximum(sums_left, sums_right), axis=1, keepdims=True)
    scale = 1.0 / largest
    one = jnp.where(r_half == c_half, 1.0, 0.0)
    for block, at in (
        (one - scale * upper, (slice(0, HALF), slice(0, HALF))),
        (-scale * corner, (slice(0, HALF), slice(HALF, BLOCK))),
        (-scale * corner_turned, (slice(HALF, BLOCK), slice(0, HALF))),
        (one - scale * lower, (slice(HALF, BLOCK), slice(HALF, BLOCK))),
    ):
        top = block.astype(BF16)
        high[at] = top
        low[at] = (block - top.astype(F32)).astype(BF16)

    row_at = lax.broadcasted_iota(jnp.int32, (16, BLOCK), 0)
    col_at = lax.broadcasted_iota(jnp.int32, (16, BLOCK), 1)
    wanted = 8 * (16 * (2 * c + lax.div(row_at, 8)) + 2 * y + b) + lax.rem(row_at, 8)
    unit = jnp.where(col_at == wanted, 1.0, 0.0)
    lead = unit
    for _ in range(7):
        lead = unit + split_dot(lead, high[...], low[...])
    result = lead * scale
    rows_out[0] = result[:8]
    rows_out[1] = result[8:]

    f_me, e_me = half_x, 4 * parity + j
    core_there = lax.rem(j, 2)

    def out_copy(n):
        i, zt = lax.div(n, 4), 4 * b + lax.rem(n, 4)
        return remote(
            rows_out.at[i], out.at[f_me, e_me], out_send.at[n], out_recv.at[f_me * 8 + e_me],
            device_at(2 * c + i, y, zt, core_there),
        )

    def out_here(n):
        return (2 * c + lax.div(n, 4) == x) & (4 * b + lax.rem(n, 4) == z) & (core_there == c)

    def send_out(n, _):
        @pl.when(jnp.logical_not(out_here(n)))
        def _():
            out_copy(n).start()

        @pl.when(out_here(n))
        def _():
            pltpu.make_async_copy(
                rows_out.at[lax.div(n, 4)], out.at[f_me, e_me], out_recv.at[f_me * 8 + e_me]
            ).start()
        return 0
    lax.fori_loop(0, 8, send_out, 0)

    def out_on(f, e):
        return remote(
            out.at[f, e], out.at[f, e], out_fwd.at[f * 4 + lax.div(e, 2)], out_recv.at[f * 8 + e],
            sibling,
        )

    def pass_out(n, _):
        copy = out_on(lax.div(n, 4), 2 * lax.rem(n, 4) + c)
        copy.wait_recv()
        copy.start()
        return 0
    lax.fori_loop(0, 8, pass_out, 0)

    def take_out(n, _):
        out_on(lax.div(n, 4), 2 * lax.rem(n, 4) + sib).wait_recv()
        return 0
    lax.fori_loop(0, 8, take_out, 0)

    for copy in (to_cross, to_cross_w, to_mate, to_mate_w, on_mate, on_mate_w):
        copy.wait_send()
    for i in range(4):
        for copy in to_sib(i):
            copy.wait_send()
    for kk in range(2):
        for bb in range(2):
            @pl.when(jnp.logical_not(z_self(kk, bb)))
            def _():
                z_copy(kk, bb).wait_send()

            @pl.when(jnp.logical_not(y2_self(kk, bb)))
            def _():
                y2_copy(kk, bb).wait_send()

        @pl.when(jnp.logical_not(diag_self(kk)))
        def _():
            diag_copy(kk).wait_send()
    for n in range(1, 8):
        y_copy(n).wait_send()

    @pl.when(sums_z)
    def _():
        def z2_left(there, _):
            @pl.when(jnp.logical_not(z2_self(there)))
            def _():
                z2_copy(there).wait_send()
            return 0
        lax.fori_loop(0, 8, z2_left, 0)

    def share_left(i, _):
        share_copy(i).wait_send()
        return 0
    lax.fori_loop(1, 16, share_left, 0)

    def share_on_left(i, _):
        share_on(i).wait_send()
        return 0
    lax.fori_loop(0, 16, share_on_left, 0)

    @pl.when(sums_diag)
    def _():
        def diag_left(k, _):
            diag_back(k).wait_send()
            return 0
        lax.fori_loop(1, 32, diag_left, 0)

    def out_left(n, _):
        @pl.when(jnp.logical_not(out_here(n)))
        def _():
            out_copy(n).wait_send()
        return 0
    lax.fori_loop(0, 8, out_left, 0)

    def out_on_left(n, _):
        out_on(lax.div(n, 4), 2 * lax.rem(n, 4) + c).wait_send()
        return 0
    lax.fori_loop(0, 8, out_on_left, 0)


def on_device(features, gradients, route_ids, gate_share, token_mask, damping):
    route = route_ids.T
    share = gate_share.reshape(1, TOKENS_HERE)
    mask = token_mask.reshape(1, TOKENS_HERE)
    damp = jnp.broadcast_to(damping.reshape(2, 1), (2, 128))
    dma = pltpu.SemaphoreType.DMA
    out = pl.pallas_call(
        refresh,
        out_shape=jax.ShapeDtypeStruct((2, 8, 8, BLOCK), F32),
        in_specs=[pl.BlockSpec(memory_space=pltpu.HBM)] * 6,
        out_specs=pl.BlockSpec(memory_space=pltpu.VMEM),
        scratch_shapes=[
            pltpu.VMEM((2, TOKENS_HERE), jnp.int32),
            pltpu.VMEM((1, TOKENS_HERE), F32),
            pltpu.VMEM((1, TOKENS_HERE), jnp.int32),
            pltpu.VMEM((2, 128), F32),
            pltpu.VMEM((8, TOKENS_HERE, BLOCK), BF16),
            pltpu.VMEM((8, 8, TOKENS_HERE), F32),
            pltpu.VMEM((TOKENS_HERE, BLOCK), BF16),
            pltpu.VMEM((8, TOKENS_HERE), F32),
            pltpu.VMEM((2, 2 * TOKENS_HERE, BLOCK), BF16),
            pltpu.VMEM((2, 3, HALF, HALF), F32),
            pltpu.VMEM((2, 16, 16, HALF), BF16),
            pltpu.VMEM((8, 2, 2, 16, HALF), BF16),
            pltpu.VMEM((2, 8, 128), F32),
            pltpu.VMEM((8, 8, 16, HALF), BF16),
            pltpu.VMEM((8, 2, 2, 16, HALF), BF16),
            pltpu.VMEM((8, 16, HALF), F32),
            pltpu.VMEM((2, 2, 16, HALF), F32),
            pltpu.VMEM((8, 16, HALF), F32),
            pltpu.VMEM((64, 8, 128), F32),
            pltpu.VMEM((2, 16, 16, HALF), F32),
            pltpu.VMEM((8, 128), F32),
            pltpu.VMEM((BLOCK, BLOCK), BF16),
            pltpu.VMEM((BLOCK, BLOCK), BF16),
            pltpu.VMEM((2, 8, BLOCK), F32),
            dma((6,)), dma((3,)), dma((8,)), dma((3,)), dma((8,)), dma((4,)), dma((4,)),
            pltpu.SemaphoreType.REGULAR,
            dma((2, 2)), dma((8,)), dma((8,)), dma((8,)), dma((8,)), dma((2, 2)), dma((8,)),
            dma((2,)), dma, dma((32,)), dma,
            dma((16,)), dma((2, 16)), dma((16,)), dma((8,)), dma((16,)), dma((8,)),
        ],
        compiler_params=pltpu.CompilerParams(
            collective_id=0, has_side_effects=True, vmem_limit_bytes=40 * 1024 * 1024
        ),
    )(features, gradients, route, share, mask, damp)
    return out[0].reshape(8, 1, 8, BLOCK), out[1].reshape(8, 1, 8, BLOCK)


def solution(mesh):
    placed = (
        P(("expert", "dp"), None),
        P(("expert", "dp"), None),
        P(("expert", "dp"), None),
        P(("expert", "dp")),
        P(("expert", "dp")),
        P("expert", None, None),
    )
    return jax.shard_map(
        on_device,
        mesh=mesh,
        in_specs=placed,
        out_specs=(P(None, None, "dp", None), P(None, None, "dp", None)),
        check_vma=False,
    )
```

time: 76.4 us -> 65.2 us (0.85)
  Pallas kernels: 71.7 us -> 60.5 us
    pallas_call x1, Pallas kernels: 71.7 us -> 60.5 us  [on_device(): pl.pallas_call(refresh, out_shape=jax.ShapeDtypeStruct((2, 8, 8, BLOCK),...]
where the time goes in v2:
time: 65.2 us; the launch traced here: 65 us
  Pallas kernels  60.5 us (93%)
  local copies, waits for them, and re-layouts  3.84 us (6%)
  between operations  0.66 us (1%)
    pallas_call x1, Pallas kernels, on_device(): pl.pallas_call(refresh, out_shape=jax.ShapeDtypeStruct((2, 8, 8, BLOCK),...  60.5 us
    unnamed x13, local copies, waits for them, and re-layouts  3.77 us

profile of v2, /device:TPU:1, one launch (start us, length us, event | category | flops | bytes accessed | tf_op | source)
XLA Modules:
  0.0 65.0 jit_solution(11441604573894001449)
XLA Ops:
  0.6 0.0 copy-start.5
  0.6 0.0 copy-start.4
  0.7 0.6 copy-done.5
  1.3 0.0 copy-start.2
  1.3 0.0 copy-start.3
  1.3 0.1 broadcast_in_dim.8.damp_in
  1.4 0.0 copy-done.4
  1.4 0.6 copy-done.2
  2.0 0.0 copy-done.3
  2.0 0.0 copy-start
  2.0 0.9 %copy-done = bf16[128,512]{1,0:T(8,128)(2,1)S(1)} copy-done((bf16[128,512]{1,0:T(8,128)(2,1)S(1)}, bf16[128,512]{1,0:T(8,128)(2,1)}, u32[]{:S(2)}) %copy-start) | copy-done | bytes 131096
  2.9 0.0 copy-start.1
  2.9 0.9 %copy-done.1 = bf16[128,512]{1,0:T(8,128)(2,1)S(1)} copy-done((bf16[128,512]{1,0:T(8,128)(2,1)S(1)}, bf16[128,512]{1,0:T(8,128)(2,1)}, u32[]{:S(2)}) %copy-start.1) | copy-done | bytes 131096
  3.8 60.5 %shard_map.77 = f32[2,8,8,512]{3,2,1,0:T(8,128)S(1)} custom-call(bf16[128,512]{1,0:T(8,128)(2,1)S(1)} %copy-done, bf16[128,512]{1,0:T(8,128)(2,1)S(1)} %copy-done.1, s32[2,128]{1,0:T(2,128)S(1)} %bitcast.12, f32[1,128]{1,0:T(1,128)S(1)} %bitcast.13, s32[1,128]{1,0:T(1,128)S(1)} %bitcast.14, f32[2,128]{1,0:T(2,128)S(1)} %broadcast_in_dim.8.damp_in), custom_call_target="tpu_custom_call" | custom-call | tf_op jit(solution)/shard_map/pallas_call | solution.py:514
  64.3 0.7 %slice_bitcast_fusion = (f32[8,1,8,512]{3,2,1,0:T(8,128)}, f32[8,1,8,512]{3,2,1,0:T(8,128)}) fusion(f32[2,8,8,512]{3,2,1,0:T(8,128)S(1)} %shard_map.77), kind=kLoop, calls=%fused_computation | loop fusion | bytes 524288
Async XLA Ops:
  0.6 0.7 %copy-start.5 = (f32[1,2,1]{1,2,0:T(1,128)S(1)}, f32[1,2,1]{1,2,0:T(1,128)}, u32[]{:S(2)}) copy-start(f32[1,2,1]{1,2,0:T(1,128)} %param.11) | copy-start | bytes 28
  0.6 0.7 %copy-start.4 = (s32[128]{0:T(128)S(1)}, s32[128]{0:T(128)}, u32[]{:S(2)}) copy-start(s32[128]{0:T(128)} %param.10) | copy-start | bytes 1540
  1.3 0.7 %copy-start.2 = (s32[128,2]{0,1:T(2,128)S(1)}, s32[128,2]{0,1:T(2,128)}, u32[]{:S(2)}) copy-start(s32[128,2]{0,1:T(2,128)} %param.8) | copy-start | bytes 3076
  1.3 0.7 %copy-start.3 = (f32[128]{0:T(128)S(1)}, f32[128]{0:T(128)}, u32[]{:S(2)}) copy-start(f32[128]{0:T(128)} %param.9) | copy-start | bytes 1540
  2.0 0.9 %copy-start = (bf16[128,512]{1,0:T(8,128)(2,1)S(1)}, bf16[128,512]{1,0:T(8,128)(2,1)}, u32[]{:S(2)}) copy-start(bf16[128,512]{1,0:T(8,128)(2,1)} %feat.1) | copy-start | bytes 393220
  2.9 0.9 %copy-start.1 = (bf16[128,512]{1,0:T(8,128)(2,1)S(1)}, bf16[128,512]{1,0:T(8,128)(2,1)}, u32[]{:S(2)}) copy-start(bf16[128,512]{1,0:T(8,128)(2,1)} %grad.1) | copy-start | bytes 393220

commit v3 on v2

v3 whole, which is shorter than its diff:
```python
import jax
import jax.numpy as jnp
from jax import lax
from jax.experimental import pallas as pl
from jax.experimental.pallas import tpu as pltpu
from jax.sharding import PartitionSpec as P

MESH = pl.DeviceIdType.MESH
BLOCK = 512
HALF = 256
TOKENS_HERE = 128
HERE_HALF = 64
LOAD_INVERSE = 1.0 / 16384.0
F32 = jnp.float32
BF16 = jnp.bfloat16


def device_at(x, y, z, c):
    return {"expert": lax.rem(z, 4) * 2 + c, "dp": x * 16 + y * 2 + lax.div(z, 4)}


def split_dot(rows, high, low):
    top = rows.astype(BF16)
    rest = (rows - top.astype(F32)).astype(BF16)
    both = jnp.concatenate([top, rest], axis=0)
    first = jnp.dot(both, high, preferred_element_type=F32)
    second = jnp.dot(top, low, preferred_element_type=F32)
    count = rows.shape[0]
    return first[:count] + (first[count:] + second)


def refresh(
    feat, grad, route_in, share_in, mask_in, damp_in, out,
    route, share, mask, damp,
    tok, wts, other, other_w, spread, gram, corners, folds, diag_out,
    by_z, by_y, z_sums, y_sums, last, diag_y, diag_mid, diag_parts,
    total, diag_total, high, low, rows_out,
    load_sem, tok_send, near_recv, sib_recv, wts_send, wts_recv, both_in,
    z_send, z_recv, y_send, y_recv, z2_send, y2_send, last_recv,
    diag_send, diag_y_recv, diag_mid_send, diag_recv, diag_back_send, diag_back_recv,
    share_send, share_recv, on_send, on_recv, out_send, out_recv, out_on_send, out_on_recv,
):
    expert_at, dp_at = lax.axis_index("expert"), lax.axis_index("dp")
    c, zl = lax.rem(expert_at, 2), lax.div(expert_at, 2)
    zh, y, x = lax.rem(dp_at, 2), lax.rem(lax.div(dp_at, 2), 8), lax.div(dp_at, 16)
    z = zh * 4 + zl
    j, b = lax.div(z, 2), lax.rem(z, 2)
    sib = 1 - c
    parity, half_x = lax.rem(x, 2), lax.div(x, 2)
    mate = x + 1 - 2 * parity
    cross = 3 - x
    row_me = b * 8 + y
    sums_diag = (y == 0) & (b == 0) & (c == 1)
    sums_z = c == lax.rem(j, 2)
    out_self = (half_x == c) & (b == zh)
    sibling = {"expert": expert_at + 1 - 2 * c, "dp": dp_at}

    def remote(src, dst, send, recv, where):
        return pltpu.make_async_remote_copy(
            src_ref=src, dst_ref=dst, send_sem=send, recv_sem=recv,
            device_id=where, device_id_type=MESH,
        )

    leaving = []

    def wait_bytes(like, sem):
        pltpu.make_async_copy(like, like, sem).wait()

    loads = (
        (route_in, route), (share_in, share), (mask_in, mask), (damp_in, damp),
    )
    for n, (src, dst) in enumerate(loads):
        pltpu.make_async_copy(src, dst, load_sem.at[n]).start()

    @pl.when(x < 2)
    def _():
        pltpu.make_async_copy(feat, tok.at[0], load_sem.at[4]).start()
        pltpu.make_async_copy(grad, other, load_sem.at[5]).start()

    @pl.when(x >= 2)
    def _():
        pltpu.make_async_copy(grad, tok.at[0], load_sem.at[4]).start()
        pltpu.make_async_copy(feat, other, load_sem.at[5]).start()

    barrier = pltpu.get_barrier_semaphore()

    def greet(where):
        pl.semaphore_signal(barrier, inc=1, device_id=where, device_id_type=MESH)

    greet(device_at(mate, y, z, c))
    greet(device_at(cross, y, z, c))
    greet(sibling)
    for n in range(1, 8):
        greet({"expert": expert_at, "dp": x * 16 + lax.rem(y + n, 8) * 2 + zh})
        greet(device_at(x, y, lax.rem(z + n, 8), c))

    for n, (src, dst) in enumerate(loads):
        pltpu.make_async_copy(src, dst, load_sem.at[n]).wait()
    lanes = lax.broadcasted_iota(jnp.int32, (8, TOKENS_HERE), 0)
    keep = jnp.broadcast_to(mask[...].astype(F32), (8, TOKENS_HERE))
    is_first = route[0:1, :] == lanes
    is_second = route[1:2, :] == lanes
    share_b = jnp.broadcast_to(share[...], (8, TOKENS_HERE))
    weight_act = jnp.where(is_first | is_second, keep, 0.0)
    weight_grad = jnp.where(is_first, share_b * keep, jnp.where(is_second, (1.0 - share_b) * keep, 0.0))

    @pl.when(x < 2)
    def _():
        wts[0] = weight_act
        other_w[...] = weight_grad

    @pl.when(x >= 2)
    def _():
        wts[0] = weight_grad
        other_w[...] = weight_act

    pltpu.make_async_copy(feat, tok.at[0], load_sem.at[4]).wait()
    pltpu.make_async_copy(grad, other, load_sem.at[5]).wait()
    pl.semaphore_wait(barrier, 17)
    pl.semaphore_signal(both_in, inc=1, device_id=sibling, device_id_type=MESH)

    at_cross, at_mate = device_at(cross, y, z, c), device_at(mate, y, z, c)

    def rows_of(ref, h):
        return ref.at[pl.ds(HERE_HALF * h, HERE_HALF)]

    def to_cross(h):
        return remote(rows_of(other, h), rows_of(tok.at[1], h), tok_send, near_recv.at[0, h], at_cross)

    def to_mate(h):
        return remote(rows_of(tok.at[0], h), rows_of(tok.at[2], h), tok_send, near_recv.at[1, h], at_mate)

    def on_mate(h):
        return remote(rows_of(tok.at[1], h), rows_of(tok.at[3], h), tok_send, near_recv.at[2, h], at_mate)

    def to_sib(i, h):
        return remote(
            rows_of(tok.at[i], h), rows_of(tok.at[4 + i], h), tok_send, sib_recv.at[i], sibling
        )

    to_cross_w = remote(other_w, wts.at[1], wts_send, wts_recv.at[0], at_cross)
    to_mate_w = remote(wts.at[0], wts.at[2], wts_send, wts_recv.at[1], at_mate)
    on_mate_w = remote(wts.at[1], wts.at[3], wts_send, wts_recv.at[2], at_mate)

    def to_sib_w(i):
        return remote(wts.at[i], wts.at[4 + i], wts_send, wts_recv.at[3 + i], sibling)

    def started(copy):
        copy.start()

    def from_sib(i):
        wait_bytes(tok.at[i], sib_recv.at[i])
        to_sib_w(i).wait_recv()

    leaving.append(lambda: wait_bytes(tok.at[pl.ds(0, 7)], tok_send))
    leaving.append(lambda: wait_bytes(wts.at[pl.ds(0, 7)], wts_send))

    def gather_gram(i, begin):
        for kk in range(2):
            e = 4 * parity + 2 * kk + c
            for h, slot in enumerate((i, 4 + i)):
                row = wts[slot, pl.ds(e, 1), :]
                column = jnp.transpose(jnp.broadcast_to(row, (TOKENS_HERE, TOKENS_HERE)))
                for q in range(4):
                    piece = tok[slot, :, 128 * q : 128 * q + 128].astype(F32) * column
                    spread[kk, 128 * h : 128 * h + 128, 128 * q : 128 * q + 128] = piece.astype(BF16)
            left, right = spread[kk, :, :HALF], spread[kk, :, HALF:]
            for n, (one, two) in enumerate(((left, right), (left, left), (right, right))):
                term = lax.dot_general(one, two, (((0,), (0,)), ((), ())), preferred_element_type=F32)
                gram[kk, n] = term if begin else gram[kk, n] + term

    started(to_cross_w)
    started(to_mate_w)
    for h in range(2):
        started(to_cross(h))
        started(to_mate(h))
    for h in range(2):
        started(to_sib(0, h))
    started(to_sib_w(0))
    to_cross_w.wait_recv()
    started(on_mate_w)
    started(to_sib_w(1))
    for h in range(2):
        to_cross(h).wait_recv()
        started(on_mate(h))
        started(to_sib(1, h))
    from_sib(0)
    gather_gram(0, True)
    to_mate_w.wait_recv()
    started(to_sib_w(2))
    for h in range(2):
        to_mate(h).wait_recv()
        started(to_sib(2, h))
    from_sib(1)
    gather_gram(1, False)
    on_mate_w.wait_recv()
    started(to_sib_w(3))
    on_mate(0).wait_recv()
    started(to_sib(3, 0))
    from_sib(2)
    gather_gram(2, False)
    on_mate(1).wait_recv()
    started(to_sib(3, 1))
    from_sib(3)
    gather_gram(3, False)

    pl.semaphore_wait(both_in, 1)

    def z_there(q):
        return 4 * lax.div(q, 2) + 2 * c + lax.rem(q, 2)

    def z_copy(q):
        return remote(
            corners.at[q], by_z.at[z], z_send, z_recv, device_at(x, y, z_there(q), c)
        )

    def y_line(there):
        return {"expert": expert_at, "dp": x * 16 + there * 2 + zh}

    def y_copy(n):
        there = lax.rem(y + n, 8)
        return remote(folds.at[there], by_y.at[y], y_send, y_recv, y_line(there))

    def own_z():
        return pltpu.make_async_copy(corners.at[2 * lax.div(z, 4) + b], by_z.at[z], z_recv)

    def own_y():
        return pltpu.make_async_copy(folds.at[y], by_y.at[y], y_recv)

    r_half = lax.broadcasted_iota(jnp.int32, (HALF, HALF), 0)
    c_half = lax.broadcasted_iota(jnp.int32, (HALF, HALF), 1)
    on_diag = r_half == c_half
    damp_row = jnp.broadcast_to(jnp.where(x < 2, damp[:, 0:1], damp[:, 1:2]), (1, 128))
    for kk in range(2):
        corners[2 * kk : 2 * kk + 2] = gram[kk, 0].astype(BF16).reshape(2, 8, 16, HALF)
        upper, lower = gram[kk, 1], gram[kk, 2]
        folded = jnp.where(r_half <= c_half, upper, lower).astype(BF16)
        folds[:, kk] = folded.reshape(8, 2, 16, HALF)
        d_up = jnp.sum(jnp.where(on_diag, upper, 0.0), axis=0, keepdims=True)
        d_low = jnp.sum(jnp.where(on_diag, lower, 0.0), axis=0, keepdims=True)
        mine = (expert_at == 4 * parity + 2 * kk + c) & (y == 0) & (zh == 0)
        diag_out[kk, 0:1] = d_up[:, :128]
        diag_out[kk, 1:2] = d_up[:, 128:]
        diag_out[kk, 2:3] = d_low[:, :128]
        diag_out[kk, 3:4] = d_low[:, 128:]
        diag_out[kk, 4:8] = jnp.broadcast_to(jnp.where(mine, damp_row, 0.0), (4, 128))

    def diag_copy():
        return remote(diag_out, diag_y.at[y], diag_send, diag_y_recv, y_line(0))

    @pl.when(y != 0)
    def _():
        diag_copy().start()

    def diag_left():
        @pl.when(y != 0)
        def _():
            diag_copy().wait_send()
    leaving.append(diag_left)

    def z_start(n):
        q = lax.rem(j + n, 4)

        @pl.when(z_there(q) != z)
        def _():
            z_copy(q).start()

    def first_left():
        wait_bytes(folds.at[pl.ds(0, 7)], y_send)

        @pl.when(sums_z)
        def _():
            wait_bytes(corners.at[pl.ds(0, 3)], z_send)

        @pl.when(jnp.logical_not(sums_z))
        def _():
            wait_bytes(corners, z_send)
    leaving.append(first_left)

    for n, ahead in enumerate(((4, 1, 7), (3, 5), (2, 6), ())):
        z_start(n)
        for m in ahead:
            started(y_copy(m))
    own_y().start()

    @pl.when(sums_z)
    def _():
        own_z().start()

    wait_bytes(by_y, y_recv)
    sum_y = by_y[0].astype(F32)
    for n in range(1, 8):
        sum_y = sum_y + by_y[n].astype(F32)
    y_sums[...] = sum_y

    def y2_copy(kk, bb):
        return remote(
            y_sums.at[kk, bb], last.at[z], y2_send, last_recv,
            device_at(x, y, 4 * kk + 2 * c + bb, 1),
        )

    def y2_self(kk, bb):
        return (c == 1) & (z == 4 * kk + 2 * c + bb)

    for kk in range(2):
        for bb in range(2):
            @pl.when(jnp.logical_not(y2_self(kk, bb)))
            def _():
                y2_copy(kk, bb).start()

            @pl.when(y2_self(kk, bb))
            def _():
                pltpu.make_async_copy(y_sums.at[kk, bb], last.at[z], last_recv).start()

    def y2_left():
        @pl.when((c == 1) & sums_z)
        def _():
            wait_bytes(last.at[pl.ds(0, 3)], y2_send)

        @pl.when(jnp.logical_not((c == 1) & sums_z))
        def _():
            wait_bytes(last.at[pl.ds(0, 4)], y2_send)
    leaving.append(y2_left)

    def diag_mid_copy(kk):
        return remote(
            diag_mid.at[kk], diag_parts.at[z], diag_mid_send.at[kk], diag_recv,
            device_at(x, 0, 4 * kk + 2 * c, 1),
        )

    def diag_self(kk):
        return (c == 1) & (z == 4 * kk + 2)

    def when_line(step):
        for kk in range(2):
            @pl.when(jnp.logical_not(diag_self(kk)))
            def _():
                step(kk)

    @pl.when(y == 0)
    def _():
        arrived = diag_y.at[pl.ds(1, 7)]
        pltpu.make_async_copy(arrived, arrived, diag_y_recv).wait()
        diag_sum = diag_out[...]
        for n in range(1, 8):
            diag_sum = diag_sum + diag_y[n]
        diag_mid[...] = diag_sum
        when_line(lambda kk: diag_mid_copy(kk).start())
        for kk in range(2):
            @pl.when(diag_self(kk))
            def _():
                pltpu.make_async_copy(diag_mid.at[kk], diag_parts.at[z], diag_recv).start()

    def diag_mid_left():
        @pl.when(y == 0)
        def _():
            when_line(lambda kk: diag_mid_copy(kk).wait_send())
    leaving.append(diag_mid_left)

    def z2_copy(there):
        return remote(
            z_sums.at[there], last.at[y], z2_send, last_recv,
            device_at(x, there, z, 0),
        )

    def z2_self(there):
        return (c == 0) & (there == y)

    @pl.when(sums_z)
    def _():
        wait_bytes(by_z, z_recv)
        sum_z = by_z[0].astype(F32)
        for n in range(1, 8):
            sum_z = sum_z + by_z[n].astype(F32)
        z_sums[...] = sum_z

        def z2_start(n, _):
            there = lax.rem(y + n, 8)

            @pl.when(jnp.logical_not(z2_self(there)))
            def _():
                z2_copy(there).start()

            @pl.when(z2_self(there))
            def _():
                pltpu.make_async_copy(z_sums.at[there], last.at[y], last_recv).start()
            return 0
        lax.fori_loop(0, 8, z2_start, 0)

    def z2_left():
        @pl.when(sums_z & (c == 0))
        def _():
            wait_bytes(z_sums.at[pl.ds(0, 7)], z2_send)

        @pl.when(sums_z & (c == 1))
        def _():
            wait_bytes(z_sums, z2_send)
    leaving.append(z2_left)

    wait_bytes(last, last_recv)
    summed = last[0]
    for n in range(1, 8):
        summed = summed + last[n]
    total[c, row_me] = summed

    def block_line(n, across):
        there = lax.rem(y + n, 8)
        return {"expert": expert_at + across * (2 - 4 * b), "dp": x * 16 + there * 2 + zh}

    def share_copy(n, across):
        own = total.at[c, row_me]
        return remote(own, own, share_send, share_recv.at[b], block_line(n, across))

    def share_on(g):
        group = total.at[c, pl.ds(8 * g, 8)]
        return remote(group, group, on_send.at[g], on_recv.at[g], sibling)

    def diag_to(where):
        return remote(diag_total, diag_total, diag_back_send, diag_back_recv, where)

    block = [(n, across) for n in (4, 3, 5, 2, 6, 1, 7) for across in (1, 0)] + [(0, 1)]
    for n, across in block:
        share_copy(n, across).start()

    @pl.when(sums_diag)
    def _():
        wait_bytes(diag_parts, diag_recv)
        diag_total[...] = jnp.sum(diag_parts[...], axis=0)
        for n, across in block:
            diag_to(block_line(n, across)).start()

    @pl.when(jnp.logical_not(sums_diag))
    def _():
        wait_bytes(diag_total, diag_back_recv)

    @pl.when(c == 1)
    def _():
        diag_to(sibling).start()

    wait_bytes(total.at[c, pl.ds(0, 7)], share_recv.at[b])
    share_on(b).start()
    wait_bytes(total.at[c, pl.ds(0, 8)], share_recv.at[1 - b])
    share_on(1 - b).start()
    for g in range(2):
        group = total.at[sib, pl.ds(8 * g, 8)]
        wait_bytes(group, on_recv.at[g])

    def share_left():
        wait_bytes(total.at[0, pl.ds(0, 15)], share_send)
        for g in range(2):
            share_on(g).wait_send()

        @pl.when(sums_diag)
        def _():
            wait_bytes(diag_y, diag_back_send)

        @pl.when((c == 1) & jnp.logical_not(sums_diag))
        def _():
            wait_bytes(diag_total, diag_back_send)
    leaving.append(share_left)

    corner = total[0].reshape(HALF, HALF) * LOAD_INVERSE
    folded = jnp.concatenate([total[1, 8 * (n % 2) + n // 2] for n in range(16)], axis=0) * LOAD_INVERSE
    turned = jnp.transpose(folded)
    damping = diag_total[4:5, :]
    d_up = jnp.concatenate(
        [diag_total[0:1] * LOAD_INVERSE + damping, diag_total[1:2] * LOAD_INVERSE + damping], axis=1
    )
    d_low = jnp.concatenate(
        [diag_total[2:3] * LOAD_INVERSE + damping, diag_total[3:4] * LOAD_INVERSE + damping], axis=1
    )
    upper = jnp.where(r_half < c_half, folded, jnp.where(r_half > c_half, turned, d_up))
    lower = jnp.where(r_half > c_half, folded, jnp.where(r_half < c_half, turned, d_low))
    corner_turned = jnp.transpose(corner)
    sums_left = jnp.sum(jnp.abs(upper) + jnp.abs(corner_turned), axis=0, keepdims=True)
    sums_right = jnp.sum(jnp.abs(corner) + jnp.abs(lower), axis=0, keepdims=True)
    largest = jnp.max(jnp.maximum(sums_left, sums_right), axis=1, keepdims=True)
    scale = 1.0 / largest
    one = jnp.where(r_half == c_half, 1.0, 0.0)
    for block, at in (
        (one - scale * upper, (slice(0, HALF), slice(0, HALF))),
        (-scale * corner, (slice(0, HALF), slice(HALF, BLOCK))),
        (-scale * corner_turned, (slice(HALF, BLOCK), slice(0, HALF))),
        (one - scale * lower, (slice(HALF, BLOCK), slice(HALF, BLOCK))),
    ):
        top = block.astype(BF16)
        high[at] = top
        low[at] = (block - top.astype(F32)).astype(BF16)

    row_at = lax.broadcasted_iota(jnp.int32, (16, BLOCK), 0)
    col_at = lax.broadcasted_iota(jnp.int32, (16, BLOCK), 1)
    wanted = 8 * (16 * (2 * c + lax.div(row_at, 8)) + 2 * y + b) + lax.rem(row_at, 8)
    unit = jnp.where(col_at == wanted, 1.0, 0.0)
    lead = unit
    for _ in range(7):
        lead = unit + split_dot(lead, high[...], low[...])
    result = lead * scale
    rows_out[0] = result[:8]
    rows_out[1] = result[8:]

    e_me = 4 * parity + j

    def out_copy(n):
        i, zt = n // 4, 4 * b + n % 4
        return remote(
            rows_out.at[i], out.at[half_x, e_me], out_send, out_recv, device_at(2 * c + i, y, zt, half_x)
        )

    def out_here(n):
        return (2 * c + n // 4 == x) & (4 * b + n % 4 == z) & (half_x == c)

    for n in range(8):
        @pl.when(jnp.logical_not(out_here(n)))
        def _():
            out_copy(n).start()

        @pl.when(out_here(n))
        def _():
            pltpu.make_async_copy(rows_out.at[n // 4], out.at[half_x, e_me], out_recv).start()

    wait_bytes(out.at[c], out_recv)
    out_on = remote(out.at[c], out.at[c], out_on_send, out_on_recv, sibling)
    out_on.start()
    wait_bytes(out.at[sib], out_on_recv)

    def out_left():
        @pl.when(out_self)
        def _():
            wait_bytes(out.at[0, pl.ds(0, 7)], out_send)

        @pl.when(jnp.logical_not(out_self))
        def _():
            wait_bytes(out.at[0], out_send)
        out_on.wait_send()
    leaving.append(out_left)

    for left in leaving:
        left()


def on_device(features, gradients, route_ids, gate_share, token_mask, damping):
    route = route_ids.T
    share = gate_share.reshape(1, TOKENS_HERE)
    mask = token_mask.reshape(1, TOKENS_HERE)
    damp = damping.reshape(1, 2)
    dma = pltpu.SemaphoreType.DMA
    out = pl.pallas_call(
        refresh,
        out_shape=jax.ShapeDtypeStruct((2, 8, 8, BLOCK), F32),
        in_specs=[pl.BlockSpec(memory_space=pltpu.HBM)] * 6,
        out_specs=pl.BlockSpec(memory_space=pltpu.VMEM),
        scratch_shapes=[
            pltpu.VMEM((2, TOKENS_HERE), jnp.int32),
            pltpu.VMEM((1, TOKENS_HERE), F32),
            pltpu.VMEM((1, TOKENS_HERE), jnp.int32),
            pltpu.VMEM((1, 2), F32),
            pltpu.VMEM((8, TOKENS_HERE, BLOCK), BF16),
            pltpu.VMEM((8, 8, TOKENS_HERE), F32),
            pltpu.VMEM((TOKENS_HERE, BLOCK), BF16),
            pltpu.VMEM((8, TOKENS_HERE), F32),
            pltpu.VMEM((2, 2 * TOKENS_HERE, BLOCK), BF16),
            pltpu.VMEM((2, 3, HALF, HALF), F32),
            pltpu.VMEM((4, 8, 16, HALF), BF16),
            pltpu.VMEM((8, 2, 2, 16, HALF), BF16),
            pltpu.VMEM((2, 8, 128), F32),
            pltpu.VMEM((8, 8, 16, HALF), BF16),
            pltpu.VMEM((8, 2, 2, 16, HALF), BF16),
            pltpu.VMEM((8, 16, HALF), F32),
            pltpu.VMEM((2, 2, 16, HALF), F32),
            pltpu.VMEM((8, 16, HALF), F32),
            pltpu.VMEM((8, 2, 8, 128), F32),
            pltpu.VMEM((2, 8, 128), F32),
            pltpu.VMEM((8, 8, 128), F32),
            pltpu.VMEM((2, 16, 16, HALF), F32),
            pltpu.VMEM((8, 128), F32),
            pltpu.VMEM((BLOCK, BLOCK), BF16),
            pltpu.VMEM((BLOCK, BLOCK), BF16),
            pltpu.VMEM((2, 8, BLOCK), F32),
            dma((6,)), dma, dma((3, 2)), dma((4,)), dma, dma((7,)), pltpu.SemaphoreType.REGULAR,
            dma, dma, dma, dma, dma, dma, dma,
            dma, dma, dma((2,)), dma, dma, dma,
            dma, dma((2,)), dma((2,)), dma((2,)), dma, dma, dma, dma,
        ],
        compiler_params=pltpu.CompilerParams(
            collective_id=0, has_side_effects=True, vmem_limit_bytes=56 * 1024 * 1024
        ),
    )(features, gradients, route, share, mask, damp)
    return out[0].reshape(8, 1, 8, BLOCK), out[1].reshape(8, 1, 8, BLOCK)


def solution(mesh):
    placed = (
        P(("expert", "dp"), None),
        P(("expert", "dp"), None),
        P(("expert", "dp"), None),
        P(("expert", "dp")),
        P(("expert", "dp")),
        P("expert", None, None),
    )
    return jax.shard_map(
        on_device,
        mesh=mesh,
        in_specs=placed,
        out_specs=(P(None, None, "dp", None), P(None, None, "dp", None)),
        check_vma=False,
    )
```

time: 65.2 us -> 60.2 us (0.923); the launches traced: 65 us -> 59.3 us
  Pallas kernels: 60.5 us -> 57 us
  local copies, waits for them, and re-layouts: 3.84 us -> 1.69 us
    pallas_call x1, Pallas kernels: 60.5 us -> 57 us  [on_device(): pl.pallas_call(refresh, out_shape=jax.ShapeDtypeStruct((2, 8, 8, BLOCK),...]
    unnamed x13 -> x1, local copies, waits for them, and re-layouts: 3.77 us -> 1.69 us
where the time goes in v3:
time: 60.2 us; the launch traced here: 59.3 us
  Pallas kernels  57 us (95%)
  local copies, waits for them, and re-layouts  1.69 us (3%)
  between operations  0.64 us (1%)
    pallas_call x1, Pallas kernels, on_device(): pl.pallas_call(refresh, out_shape=jax.ShapeDtypeStruct((2, 8, 8, BLOCK),...  57 us
    unnamed x1, local copies, waits for them, and re-layouts  1.69 us

profile of v3, /device:TPU:1, one launch (start us, length us, event | category | flops | bytes accessed | tf_op | source)
XLA Modules:
  0.0 59.3 jit_solution(840480540785048638)
XLA Ops:
  0.6 57.0 %shard_map.77 = f32[2,8,8,512]{3,2,1,0:T(8,128)} custom-call(bf16[128,512]{1,0:T(8,128)(2,1)} %feat.1, bf16[128,512]{1,0:T(8,128)(2,1)} %grad.1, s32[2,128]{1,0:T(2,128)} %bitcast.12, f32[1,128]{1,0:T(1,128)} %bitcast.13, s32[1,128]{1,0:T(1,128)} %bitcast.14, f32[1,2]{1,0:T(1,128)} %bitcast.15), custom_call_target="tpu_custom_call" | custom-call | tf_op jit(solution)/shard_map/pallas_call | solution.py:547
  57.7 1.7 %slice_bitcast_fusion = (f32[8,1,8,512]{3,2,1,0:T(8,128)}, f32[8,1,8,512]{3,2,1,0:T(8,128)}) fusion(f32[2,8,8,512]{3,2,1,0:T(8,128)} %shard_map.77), kind=kLoop, calls=%fused_computation | loop fusion | bytes 524288

commit v4 on v3

--- a/solution.py
+++ b/solution.py
@@ -35,7 +35,8 @@
     tok, wts, other, other_w, spread, gram, corners, folds, diag_out,
     by_z, by_y, z_sums, y_sums, last, diag_y, diag_mid, diag_parts,
     total, diag_total, high, low, rows_out,
-    load_sem, tok_send, near_recv, sib_recv, wts_send, wts_recv, both_in,
+    load_sem, tok_send, near_recv, sib_recv, wts_send, wts_recv,
+    near_in, lines_in, both_in, cross_in, mate_in,
     z_send, z_recv, y_send, y_recv, z2_send, y2_send, last_recv,
     diag_send, diag_y_recv, diag_mid_send, diag_recv, diag_back_send, diag_back_recv,
     share_send, share_recv, on_send, on_recv, out_send, out_recv, out_on_send, out_on_recv,
@@ -84,15 +85,21 @@
 
     barrier = pltpu.get_barrier_semaphore()
 
-    def greet(where):
-        pl.semaphore_signal(barrier, inc=1, device_id=where, device_id_type=MESH)
-
-    greet(device_at(mate, y, z, c))
-    greet(device_at(cross, y, z, c))
-    greet(sibling)
-    for n in range(1, 8):
-        greet({"expert": expert_at, "dp": x * 16 + lax.rem(y + n, 8) * 2 + zh})
-        greet(device_at(x, y, lax.rem(z + n, 8), c))
+    def y_line(there):
+        return {"expert": expert_at, "dp": x * 16 + there * 2 + zh}
+
+    def near(step):
+        return (
+            y_line(lax.rem(y + step, 8)), y_line(lax.rem(y + 8 - step, 8)),
+            device_at(x, y, lax.rem(z + step, 8), c), device_at(x, y, lax.rem(z + 8 - step, 8), c),
+        )
+
+    def tell(sem, where):
+        pl.semaphore_signal(sem, inc=1, device_id=where, device_id_type=MESH)
+
+    at_cross, at_mate = device_at(cross, y, z, c), device_at(mate, y, z, c)
+    for where in (at_cross, at_mate, *near(1), sibling):
+        tell(barrier, where)
 
     for n, (src, dst) in enumerate(loads):
         pltpu.make_async_copy(src, dst, load_sem.at[n]).wait()
@@ -116,10 +123,8 @@
 
     pltpu.make_async_copy(feat, tok.at[0], load_sem.at[4]).wait()
     pltpu.make_async_copy(grad, other, load_sem.at[5]).wait()
-    pl.semaphore_wait(barrier, 17)
-    pl.semaphore_signal(both_in, inc=1, device_id=sibling, device_id_type=MESH)
-
-    at_cross, at_mate = device_at(cross, y, z, c), device_at(mate, y, z, c)
+    pl.semaphore_wait(barrier, 7)
+
 
     def rows_of(ref, h):
         return ref.at[pl.ds(HERE_HALF * h, HERE_HALF)]
@@ -177,6 +182,8 @@
     for h in range(2):
         started(to_sib(0, h))
     started(to_sib_w(0))
+    for where in near(1):
+        tell(near_in, where)
     to_cross_w.wait_recv()
     started(on_mate_w)
     started(to_sib_w(1))
@@ -191,6 +198,9 @@
     for h in range(2):
         to_mate(h).wait_recv()
         started(to_sib(2, h))
+    pl.semaphore_wait(near_in, 4)
+    for where in near(2):
+        tell(lines_in, where)
     from_sib(1)
     gather_gram(1, False)
     on_mate_w.wait_recv()
@@ -204,7 +214,8 @@
     from_sib(3)
     gather_gram(3, False)
 
-    pl.semaphore_wait(both_in, 1)
+    pl.semaphore_wait(lines_in, 4)
+    tell(both_in, sibling)
 
     def z_there(q):
         return 4 * lax.div(q, 2) + 2 * c + lax.rem(q, 2)
@@ -213,9 +224,6 @@
         return remote(
             corners.at[q], by_z.at[z], z_send, z_recv, device_at(x, y, z_there(q), c)
         )
-
-    def y_line(there):
-        return {"expert": expert_at, "dp": x * 16 + there * 2 + zh}
 
     def y_copy(n):
         there = lax.rem(y + n, 8)
@@ -287,6 +295,9 @@
     def _():
         own_z().start()
 
+    pl.semaphore_wait(both_in, 1)
+    tell(cross_in, at_cross)
+    tell(cross_in, at_mate)
     wait_bytes(by_y, y_recv)
     sum_y = by_y[0].astype(F32)
     for n in range(1, 8):
@@ -418,6 +429,8 @@
     def diag_to(where):
         return remote(diag_total, diag_total, diag_back_send, diag_back_recv, where)
 
+    pl.semaphore_wait(cross_in, 2)
+    tell(mate_in, at_mate)
     block = [(n, across) for n in (4, 3, 5, 2, 6, 1, 7) for across in (1, 0)] + [(0, 1)]
     for n, across in block:
         share_copy(n, across).start()
@@ -498,6 +511,7 @@
     rows_out[0] = result[:8]
     rows_out[1] = result[8:]
 
+    pl.semaphore_wait(mate_in, 1)
     e_me = 4 * parity + j
 
     def out_copy(n):
@@ -576,15 +590,16 @@
             pltpu.VMEM((BLOCK, BLOCK), BF16),
             pltpu.VMEM((BLOCK, BLOCK), BF16),
             pltpu.VMEM((2, 8, BLOCK), F32),
-            dma((6,)), dma, dma((3, 2)), dma((4,)), dma, dma((7,)), pltpu.SemaphoreType.REGULAR,
+            dma((6,)), dma, dma((3, 2)), dma((4,)), dma, dma((7,)),
+            *[pltpu.SemaphoreType.REGULAR] * 5,
             dma, dma, dma, dma, dma, dma, dma,
             dma, dma, dma((2,)), dma, dma, dma,
             dma, dma((2,)), dma((2,)), dma((2,)), dma, dma, dma, dma,
         ],
         compiler_params=pltpu.CompilerParams(
-            collective_id=0, has_side_effects=True, vmem_limit_bytes=56 * 1024 * 1024
+            collective_id=0, has_side_effects=True, vmem_limit_bytes=40 * 1024 * 1024
         ),
-    )(features, gradients, route, share, mask, damp)
+    )(*[pltpu.with_memory_space_constraint(a, pltpu.HBM) for a in (features, gradients, route, share, mask, damp)])
     return out[0].reshape(8, 1, 8, BLOCK), out[1].reshape(8, 1, 8, BLOCK)
 
 

time: 60.2 us -> 57.5 us (0.955); the launches traced: 59.3 us -> 57.4 us
  Pallas kernels: 57 us -> 56 us
  local copies, waits for them, and re-layouts: 1.69 us -> 0.72 us
    pallas_call x1, Pallas kernels: 57 us -> 56 us  [on_device(): pl.pallas_call(refresh, out_shape=jax.ShapeDtypeStruct((2, 8, 8, BLOCK),...]
    unnamed x1, local copies, waits for them, and re-layouts: 1.69 us -> 0.72 us
where the time goes in v4:
time: 57.5 us; the launch traced here: 57.4 us
  Pallas kernels  56 us (97%)
  local copies, waits for them, and re-layouts  0.72 us (1%)
  between operations  0.64 us (1%)
    pallas_call x1, Pallas kernels, on_device(): pl.pallas_call(refresh, out_shape=jax.ShapeDtypeStruct((2, 8, 8, BLOCK),...  56 us

profile of v4, /device:TPU:1, one launch (start us, length us, event | category | flops | bytes accessed | tf_op | source)
XLA Modules:
  0.0 57.4 jit_solution(7534180459747400433)
XLA Ops:
  0.6 56.0 %shard_map.77 = f32[2,8,8,512]{3,2,1,0:T(8,128)S(1)} custom-call(bf16[128,512]{1,0:T(8,128)(2,1)} %feat.1, bf16[128,512]{1,0:T(8,128)(2,1)} %grad.1, s32[2,128]{1,0:T(2,128)} %bitcast.12, f32[1,128]{1,0:T(1,128)} %bitcast.13, s32[1,128]{1,0:T(1,128)} %bitcast.14, f32[1,2]{1,0:T(1,128)} %bitcast.15), custom_call_target="tpu_custom_call" | custom-call | tf_op jit(solution)/shard_map/pallas_call | solution.py:561
  56.6 0.7 %slice_bitcast_fusion = (f32[8,1,8,512]{3,2,1,0:T(8,128)}, f32[8,1,8,512]{3,2,1,0:T(8,128)}) fusion(f32[2,8,8,512]{3,2,1,0:T(8,128)S(1)} %shard_map.77), kind=kLoop, calls=%fused_computation | loop fusion | bytes 524288

commit v5 on v4

--- a/solution.py
+++ b/solution.py
@@ -84,21 +84,30 @@
         pltpu.make_async_copy(feat, other, load_sem.at[5]).start()
 
     barrier = pltpu.get_barrier_semaphore()
+    z_end, y_end = (z == 3) | (z == 4), (y == 3) | (y == 4)
+    ends = z_end.astype(jnp.int32) + y_end.astype(jnp.int32)
 
     def y_line(there):
         return {"expert": expert_at, "dp": x * 16 + there * 2 + zh}
 
-    def near(step):
-        return (
-            y_line(lax.rem(y + step, 8)), y_line(lax.rem(y + 8 - step, 8)),
-            device_at(x, y, lax.rem(z + step, 8), c), device_at(x, y, lax.rem(z + 8 - step, 8), c),
-        )
-
     def tell(sem, where):
         pl.semaphore_signal(sem, inc=1, device_id=where, device_id_type=MESH)
 
+    z_four = [{"expert": lax.rem(zl + n, 4) * 2 + c, "dp": dp_at} for n in range(1, 4)]
+    y_four = [y_line(4 * lax.div(y, 4) + lax.rem(y + n, 4)) for n in range(1, 4)]
     at_cross, at_mate = device_at(cross, y, z, c), device_at(mate, y, z, c)
-    for where in (at_cross, at_mate, *near(1), sibling):
+
+    def tell_over(sem):
+        @pl.when(z_end)
+        def _():
+            tell(sem, device_at(x, y, 7 - z, c))
+
+        @pl.when(y_end)
+        def _():
+            tell(sem, y_line(7 - y))
+
+    tell_over(barrier)
+    for where in (*z_four, *y_four, at_cross, at_mate, sibling):
         tell(barrier, where)
 
     for n, (src, dst) in enumerate(loads):
@@ -123,7 +132,8 @@
 
     pltpu.make_async_copy(feat, tok.at[0], load_sem.at[4]).wait()
     pltpu.make_async_copy(grad, other, load_sem.at[5]).wait()
-    pl.semaphore_wait(barrier, 7)
+    pl.semaphore_wait(barrier, 9 + ends)
+    tell_over(near_in)
 
 
     def rows_of(ref, h):
@@ -182,8 +192,6 @@
     for h in range(2):
         started(to_sib(0, h))
     started(to_sib_w(0))
-    for where in near(1):
-        tell(near_in, where)
     to_cross_w.wait_recv()
     started(on_mate_w)
     started(to_sib_w(1))
@@ -191,6 +199,20 @@
         to_cross(h).wait_recv()
         started(on_mate(h))
         started(to_sib(1, h))
+
+    @pl.when(ends > 0)
+    def _():
+        pl.semaphore_wait(near_in, ends)
+
+    @pl.when(z_end)
+    def _():
+        for where in z_four:
+            tell(lines_in, where)
+
+    @pl.when(y_end)
+    def _():
+        for where in y_four:
+            tell(lines_in, where)
     from_sib(0)
     gather_gram(0, True)
     to_mate_w.wait_recv()
@@ -198,9 +220,6 @@
     for h in range(2):
         to_mate(h).wait_recv()
         started(to_sib(2, h))
-    pl.semaphore_wait(near_in, 4)
-    for where in near(2):
-        tell(lines_in, where)
     from_sib(1)
     gather_gram(1, False)
     on_mate_w.wait_recv()
@@ -214,7 +233,9 @@
     from_sib(3)
     gather_gram(3, False)
 
-    pl.semaphore_wait(lines_in, 4)
+    @pl.when(ends < 2)
+    def _():
+        pl.semaphore_wait(lines_in, 2 - ends)
     tell(both_in, sibling)
 
     def z_there(q):
@@ -504,8 +525,13 @@
     col_at = lax.broadcasted_iota(jnp.int32, (16, BLOCK), 1)
     wanted = 8 * (16 * (2 * c + lax.div(row_at, 8)) + 2 * y + b) + lax.rem(row_at, 8)
     unit = jnp.where(col_at == wanted, 1.0, 0.0)
-    lead = unit
-    for _ in range(7):
+    here = []
+    for i in range(2):
+        rows = pl.ds(pl.multiple_of(16 * (8 * (2 * c + i) + y), 16), 16)
+        both = high[rows, :].astype(F32) + low[rows, :].astype(F32)
+        here.append(jnp.where(b == 0, both[:8], both[8:]))
+    lead = unit + jnp.concatenate(here, axis=0)
+    for _ in range(6):
         lead = unit + split_dot(lead, high[...], low[...])
     result = lead * scale
     rows_out[0] = result[:8]

time: 57.5 us -> 56.6 us (0.984)
  Pallas kernels: 56 us -> 55 us
    pallas_call x1, Pallas kernels: 56 us -> 55 us  [on_device(): pl.pallas_call(refresh, out_shape=jax.ShapeDtypeStruct((2, 8, 8, BLOCK),...]
where the time goes in v5:
time: 56.6 us; the launch traced here: 56.4 us
  Pallas kernels  55 us (97%)
  local copies, waits for them, and re-layouts  0.72 us (1%)
  between operations  0.64 us (1%)
    pallas_call x1, Pallas kernels, on_device(): pl.pallas_call(refresh, out_shape=jax.ShapeDtypeStruct((2, 8, 8, BLOCK),...  55 us

profile of v5, /device:TPU:1, one launch (start us, length us, event | category | flops | bytes accessed | tf_op | source)
XLA Modules:
  0.0 56.4 jit_solution(3368440563397282615)
XLA Ops:
  0.6 55.0 %shard_map.77 = f32[2,8,8,512]{3,2,1,0:T(8,128)S(1)} custom-call(bf16[128,512]{1,0:T(8,128)(2,1)} %feat.1, bf16[128,512]{1,0:T(8,128)(2,1)} %grad.1, s32[2,128]{1,0:T(2,128)} %bitcast.12, f32[1,128]{1,0:T(1,128)} %bitcast.13, s32[1,128]{1,0:T(1,128)} %bitcast.14, f32[1,2]{1,0:T(1,128)} %bitcast.15), custom_call_target="tpu_custom_call" | custom-call | tf_op jit(solution)/shard_map/pallas_call | solution.py:587
  55.7 0.7 %slice_bitcast_fusion = (f32[8,1,8,512]{3,2,1,0:T(8,128)}, f32[8,1,8,512]{3,2,1,0:T(8,128)}) fusion(f32[2,8,8,512]{3,2,1,0:T(8,128)S(1)} %shard_map.77), kind=kLoop, calls=%fused_computation | loop fusion | bytes 524288

commit v6 on v5

--- a/solution.py
+++ b/solution.py
@@ -9,7 +9,8 @@
 BLOCK = 512
 HALF = 256
 TOKENS_HERE = 128
-HERE_HALF = 64
+HERE_PART = 32
+PARTS = 4
 LOAD_INVERSE = 1.0 / 16384.0
 F32 = jnp.float32
 BF16 = jnp.bfloat16
@@ -137,7 +138,7 @@
 
 
     def rows_of(ref, h):
-        return ref.at[pl.ds(HERE_HALF * h, HERE_HALF)]
+        return ref.at[pl.ds(HERE_PART * h, HERE_PART)]
 
     def to_cross(h):
         return remote(rows_of(other, h), rows_of(tok.at[1], h), tok_send, near_recv.at[0, h], at_cross)
@@ -186,16 +187,16 @@
 
     started(to_cross_w)
     started(to_mate_w)
-    for h in range(2):
+    for h in range(PARTS):
         started(to_cross(h))
         started(to_mate(h))
-    for h in range(2):
+    for h in range(PARTS):
         started(to_sib(0, h))
     started(to_sib_w(0))
     to_cross_w.wait_recv()
     started(on_mate_w)
     started(to_sib_w(1))
-    for h in range(2):
+    for h in range(PARTS):
         to_cross(h).wait_recv()
         started(on_mate(h))
         started(to_sib(1, h))
@@ -217,19 +218,20 @@
     gather_gram(0, True)
     to_mate_w.wait_recv()
     started(to_sib_w(2))
-    for h in range(2):
+    for h in range(PARTS):
         to_mate(h).wait_recv()
         started(to_sib(2, h))
     from_sib(1)
     gather_gram(1, False)
     on_mate_w.wait_recv()
     started(to_sib_w(3))
-    on_mate(0).wait_recv()
-    started(to_sib(3, 0))
+    for h in range(PARTS - 1):
+        on_mate(h).wait_recv()
+        started(to_sib(3, h))
     from_sib(2)
     gather_gram(2, False)
-    on_mate(1).wait_recv()
-    started(to_sib(3, 1))
+    on_mate(PARTS - 1).wait_recv()
+    started(to_sib(3, PARTS - 1))
     from_sib(3)
     gather_gram(3, False)
 
@@ -334,7 +336,8 @@
     def y2_self(kk, bb):
         return (c == 1) & (z == 4 * kk + 2 * c + bb)
 
-    for kk in range(2):
+    for far in range(2):
+        kk = (1 - lax.div(z, 4)) if far == 0 else lax.div(z, 4)
         for bb in range(2):
             @pl.when(jnp.logical_not(y2_self(kk, bb)))
             def _():
@@ -353,6 +356,34 @@
         def _():
             wait_bytes(last.at[pl.ds(0, 4)], y2_send)
     leaving.append(y2_left)
+
+    def z2_copy(there):
+        return remote(
+            z_sums.at[there], last.at[y], z2_send, last_recv,
+            device_at(x, there, z, 0),
+        )
+
+    def z2_self(there):
+        return (c == 0) & (there == y)
+
+    @pl.when(sums_z)
+    def _():
+        wait_bytes(by_z, z_recv)
+        sum_z = by_z[0].astype(F32)
+        for n in range(1, 8):
+            sum_z = sum_z + by_z[n].astype(F32)
+        z_sums[...] = sum_z
+
+        for n in (4, 3, 5, 2, 6, 1, 7, 0):
+            there = lax.rem(y + n, 8)
+
+            @pl.when(jnp.logical_not(z2_self(there)))
+            def _():
+                z2_copy(there).start()
+
+            @pl.when(z2_self(there))
+            def _():
+                pltpu.make_async_copy(z_sums.at[there], last.at[y], last_recv).start()
 
     def diag_mid_copy(kk):
         return remote(
@@ -388,36 +419,6 @@
         def _():
             when_line(lambda kk: diag_mid_copy(kk).wait_send())
     leaving.append(diag_mid_left)
-
-    def z2_copy(there):
-        return remote(
-            z_sums.at[there], last.at[y], z2_send, last_recv,
-            device_at(x, there, z, 0),
-        )
-
-    def z2_self(there):
-        return (c == 0) & (there == y)
-
-    @pl.when(sums_z)
-    def _():
-        wait_bytes(by_z, z_recv)
-        sum_z = by_z[0].astype(F32)
-        for n in range(1, 8):
-            sum_z = sum_z + by_z[n].astype(F32)
-        z_sums[...] = sum_z
-
-        def z2_start(n, _):
-            there = lax.rem(y + n, 8)
-
-            @pl.when(jnp.logical_not(z2_self(there)))
-            def _():
-                z2_copy(there).start()
-
-            @pl.when(z2_self(there))
-            def _():
-                pltpu.make_async_copy(z_sums.at[there], last.at[y], last_recv).start()
-            return 0
-        lax.fori_loop(0, 8, z2_start, 0)
 
     def z2_left():
         @pl.when(sums_z & (c == 0))
@@ -616,7 +617,7 @@
             pltpu.VMEM((BLOCK, BLOCK), BF16),
             pltpu.VMEM((BLOCK, BLOCK), BF16),
             pltpu.VMEM((2, 8, BLOCK), F32),
-            dma((6,)), dma, dma((3, 2)), dma((4,)), dma, dma((7,)),
+            dma((6,)), dma, dma((3, PARTS)), dma((4,)), dma, dma((7,)),
             *[pltpu.SemaphoreType.REGULAR] * 5,
             dma, dma, dma, dma, dma, dma, dma,
             dma, dma, dma((2,)), dma, dma, dma,

time: 56.6 us -> 56.2 us (level)
  no operation moved by 1% of the time
where the time goes in v6:
time: 56.2 us; the launch traced here: 56 us
  Pallas kernels  54.6 us (97%)
  local copies, waits for them, and re-layouts  0.72 us (1%)
  between operations  0.64 us (1%)
    pallas_call x1, Pallas kernels, on_device(): pl.pallas_call(refresh, out_shape=jax.ShapeDtypeStruct((2, 8, 8, BLOCK),...  54.6 us

profile of v6, /device:TPU:1, one launch (start us, length us, event | category | flops | bytes accessed | tf_op | source)
XLA Modules:
  0.0 56.0 jit_solution(11364086390101106157)
XLA Ops:
  0.6 54.6 %shard_map.77 = f32[2,8,8,512]{3,2,1,0:T(8,128)S(1)} custom-call(bf16[128,512]{1,0:T(8,128)(2,1)} %feat.1, bf16[128,512]{1,0:T(8,128)(2,1)} %grad.1, s32[2,128]{1,0:T(2,128)} %bitcast.12, f32[1,128]{1,0:T(1,128)} %bitcast.13, s32[1,128]{1,0:T(1,128)} %bitcast.14, f32[1,2]{1,0:T(1,128)} %bitcast.15), custom_call_target="tpu_custom_call" | custom-call | tf_op jit(solution)/shard_map/pallas_call | solution.py:588
  55.3 0.7 %slice_bitcast_fusion = (f32[8,1,8,512]{3,2,1,0:T(8,128)}, f32[8,1,8,512]{3,2,1,0:T(8,128)}) fusion(f32[2,8,8,512]{3,2,1,0:T(8,128)S(1)} %shard_map.77), kind=kLoop, calls=%fused_computation | loop fusion | bytes 524288

commit v7 on v6

--- a/solution.py
+++ b/solution.py
@@ -189,6 +189,7 @@
     started(to_mate_w)
     for h in range(PARTS):
         started(to_cross(h))
+    for h in range(PARTS):
         started(to_mate(h))
     for h in range(PARTS):
         started(to_sib(0, h))

time: 56.2 us -> 56.2 us (level)
  no operation moved by 1% of the time
where the time goes in v7:
time: 56.2 us; the launch traced here: 56 us
  Pallas kernels  54.6 us (97%)
  local copies, waits for them, and re-layouts  0.72 us (1%)
  between operations  0.64 us (1%)
    pallas_call x1, Pallas kernels, on_device(): pl.pallas_call(refresh, out_shape=jax.ShapeDtypeStruct((2, 8, 8, BLOCK),...  54.6 us

profile of v7, /device:TPU:1, one launch (start us, length us, event | category | flops | bytes accessed | tf_op | source)
XLA Modules:
  0.0 56.0 jit_solution(1846227421586418159)
XLA Ops:
  0.6 54.6 %shard_map.77 = f32[2,8,8,512]{3,2,1,0:T(8,128)S(1)} custom-call(bf16[128,512]{1,0:T(8,128)(2,1)} %feat.1, bf16[128,512]{1,0:T(8,128)(2,1)} %grad.1, s32[2,128]{1,0:T(2,128)} %bitcast.12, f32[1,128]{1,0:T(1,128)} %bitcast.13, s32[1,128]{1,0:T(1,128)} %bitcast.14, f32[1,2]{1,0:T(1,128)} %bitcast.15), custom_call_target="tpu_custom_call" | custom-call | tf_op jit(solution)/shard_map/pallas_call | solution.py:589
  55.3 0.7 %slice_bitcast_fusion = (f32[8,1,8,512]{3,2,1,0:T(8,128)}, f32[8,1,8,512]{3,2,1,0:T(8,128)}) fusion(f32[2,8,8,512]{3,2,1,0:T(8,128)S(1)} %shard_map.77), kind=kLoop, calls=%fused_computation | loop fusion | bytes 524288
